TPU v7x, 32 devices: a whole 2x2x4 slice. The times are simulated.
32 devices in a mesh: rows: 4 (over y, x), feat: 8 (over z, core).
Axes of the slice: x: 2, y: 2, z: 4, core: 2. Of those that a mesh axis runs over, the one named last changes fastest.
Arguments:
- pool_a: bfloat16 [5120, 9216], P('rows', 'feat'), may hold values from -6 to 6
- pool_b: bfloat16 [5120, 9216], P('rows', 'feat'), may hold values from -6 to 6
- weight_a: bfloat16 [9216, 4096], P('feat'), may hold values from -0.09375 to 0.09375
- weight_b: bfloat16 [9216, 4096], P('feat'), may hold values from -0.09375 to 0.09375
- bias_a: float32 [4096], P('feat'), may hold values from -3 to 3
- bias_b: float32 [4096], P('feat'), may hold values from -3 to 3
- stitch: float32 [2, 2, 4096], P(None, None, 'feat'), may hold values from 0.1 to 1
- crop_count: int32 [5120], P('rows'), may hold values from 1 to 4
- row_mask: int32 [5120], P('rows'), may hold values from 0 to 1, as said below
- outgrad_a: bfloat16 [5120, 4096], P('rows', 'feat'), may hold values from -6 to 6
- outgrad_b: bfloat16 [5120, 4096], P('rows', 'feat'), may hold values from -6 to 6
Outputs:
- mixed_a: bfloat16 [5120, 4096], P('rows', 'feat')
- mixed_b: bfloat16 [5120, 4096], P('rows', 'feat')
- pool_grad_a: bfloat16 [5120, 9216], P('rows', 'feat')
- pool_grad_b: bfloat16 [5120, 9216], P('rows', 'feat')
- weight_grad_a: float32 [9216, 4096], P('feat', 'rows')
- weight_grad_b: float32 [9216, 4096], P('feat', 'rows')
- bias_grad_a: float32 [4096], P(('feat', 'rows'))
- bias_grad_b: float32 [4096], P(('feat', 'rows'))
- stitch_grad: float32 [2, 2, 4096], P(None, None, ('feat', 'rows'))
Inputs may be any that keep to these rules, and one draw needn't show every extreme that they name: `row_mask`: in each aligned block of 1280 rows (the rows of one device) the rows with mask 1 come first and fill half of the block or more; some block is all ones.
All inputs are finite; a program needn't handle non-finite values.
Results may differ from a plain program's by a relative error of at most 0.017.
Values may be sent and summed in bfloat16 or wider, within the bound.
A program may use at most 256 MiB of HBM per device.

v0:
```python
import jax
import jax.numpy as jnp
from jax import lax
from jax.sharding import PartitionSpec as P


def shards(
    pool_a,
    pool_b,
    weight_a,
    weight_b,
    bias_a,
    bias_b,
    stitch,
    crop_count,
    row_mask,
    outgrad_a,
    outgrad_b,
):
    rows_here = pool_a.shape[0]
    local_ch = bias_a.shape[0]
    row_scale = row_mask.astype(jnp.float32) / crop_count.astype(jnp.float32)
    contract_first = (((0,), (1,)), ((), ()))

    def partial_term(count):
        width = count // 2
        part_a = lax.dot_general(
            weight_a, pool_a, contract_first, preferred_element_type=jnp.float32
        )
        part_b = lax.dot_general(
            weight_b, pool_b, contract_first, preferred_element_type=jnp.float32
        )
        return jnp.stack([part_a, part_b], axis=1).reshape(2 * width, rows_here)

    biases = jnp.stack([bias_a, bias_b], axis=1)[:, :, None]

    def local_forward(pre_both, stitch_w):
        act = jax.nn.gelu(pre_both, approximate=False)
        act_a = act[:, 0]
        act_b = act[:, 1]
        coef = stitch_w[:, :, :, None]
        out_a = coef[0, 0] * act_a + coef[0, 1] * act_b
        out_b = coef[1, 0] * act_a + coef[1, 1] * act_b
        return jnp.stack([out_a, out_b], axis=1) * row_scale

    summed = lax.psum_scatter(
        partial_term(2 * local_ch * lax.axis_size("feat")).astype(jnp.bfloat16),
        "feat",
        scatter_dimension=0,
        tiled=True,
    ).astype(jnp.float32)
    pre_both = summed.reshape(local_ch, 2, rows_here) + biases
    mixed = local_forward(pre_both, stitch)
    summed_again = lax.psum_scatter(
        partial_term(2 * local_ch * lax.axis_size("feat")).astype(jnp.bfloat16),
        "feat",
        scatter_dimension=0,
        tiled=True,
    ).astype(jnp.float32)
    pre_back = summed_again.reshape(local_ch, 2, rows_here) + biases
    unused, pull = jax.vjp(local_forward, pre_back, stitch)
    cotangent = jnp.stack([outgrad_a.T, outgrad_b.T], axis=1).astype(jnp.float32)
    grad_pre, grad_stitch = pull(cotangent)
    grad_low = grad_pre.astype(jnp.bfloat16)
    grad_bias = jnp.sum(grad_low.astype(jnp.float32), axis=2).T
    piece = lax.all_gather(grad_low, "feat", axis=0, tiled=True)
    width = piece.shape[0]
    piece_a = piece[:, 0, :]
    piece_b = piece[:, 1, :]
    back_a = lax.dot_general(piece_a, weight_a, contract_first, preferred_element_type=jnp.float32)
    back_b = lax.dot_general(piece_b, weight_b, contract_first, preferred_element_type=jnp.float32)
    wgrad_a = lax.dot_general(pool_a, piece_a, contract_first, preferred_element_type=jnp.float32)
    wgrad_b = lax.dot_general(pool_b, piece_b, contract_first, preferred_element_type=jnp.float32)
    pool_acc = jnp.stack([back_a, back_b], axis=0)
    weight_acc = jnp.stack([wgrad_a, wgrad_b], axis=0)
    weight_sums, bias_sums, stitch_sums = (
        lax.psum_scatter(
            weight_acc.astype(jnp.bfloat16), "rows", scatter_dimension=2, tiled=True
        ).astype(jnp.float32),
        lax.psum_scatter(
            grad_bias.astype(jnp.bfloat16), "rows", scatter_dimension=1, tiled=True
        ).astype(jnp.float32),
        lax.psum_scatter(
            grad_stitch.astype(jnp.bfloat16), "rows", scatter_dimension=2, tiled=True
        ).astype(jnp.float32),
    )
    mixed_a = mixed[:, 0, :].T.astype(jnp.bfloat16)
    mixed_b = mixed[:, 1, :].T.astype(jnp.bfloat16)
    pool_grad_a = pool_acc[0].astype(jnp.bfloat16)
    pool_grad_b = pool_acc[1].astype(jnp.bfloat16)
    return (
        mixed_a,
        mixed_b,
        pool_grad_a,
        pool_grad_b,
        weight_sums[0],
        weight_sums[1],
        bias_sums[0],
        bias_sums[1],
        stitch_sums,
    )


def solution(mesh):
    return jax.shard_map(
        shards,
        mesh=mesh,
        in_specs=(
            P("rows", "feat"),
            P("rows", "feat"),
            P("feat", None),
            P("feat", None),
            P("feat"),
            P("feat"),
            P(None, None, "feat"),
            P("rows"),
            P("rows"),
            P("rows", "feat"),
            P("rows", "feat"),
        ),
        out_specs=(
            P("rows", "feat"),
            P("rows", "feat"),
            P("rows", "feat"),
            P("rows", "feat"),
            P("feat", "rows"),
            P("feat", "rows"),
            P(("feat", "rows")),
            P(("feat", "rows")),
            P(None, None, ("feat", "rows")),
        ),
        check_vma=False,
    )
```

profile of v0, /device:TPU:0, one launch (start us, length us, event | category | flops | bytes accessed | tf_op | source)
XLA Modules:
  0.0 963.6 jit_solution(5138877182561113812)
XLA Ops:
  7.2 0.0 copy-start
  7.2 0.0 reduce-scatter.9.cloned.1.call-start
  7.2 0.0 copy-start.8
  7.2 19.8 %fusion = bf16[4096,1,1280]{2,0,1:T(8,128)(2,1)} fusion(bf16[1152,4096]{1,0:T(8,128)(2,1)} %param.13, bf16[1280,1152]{1,0:T(8,128)(2,1)} %param.11), kind=kOutput, calls=%fused_computation.6 | convolution fusion | flops 12084838400 | bytes 22872064 | tf_op jit(solution)/shard_map/dot_general | solution.py:27
  27.1 0.0 copy-done
  27.1 0.0 copy-done.8
  27.1 16.1 %fusion.1 = bf16[4096,1,1280]{2,0,1:T(8,128)(2,1)} fusion(bf16[1152,4096]{1,0:T(8,128)(2,1)S(1)} %copy-done.8, bf16[1280,1152]{1,0:T(8,128)(2,1)S(1)} %copy-done), kind=kOutput, calls=%fused_computation.7 | convolution fusion | flops 12084838400 | bytes 22872064 | tf_op jit(solution)/shard_map/dot_general | solution.py:30
  43.1 10.0 %pad_maximum_fusion = bf16[4096,2,1280]{2,0,1:T(8,128)(2,1)S(1)} fusion(bf16[4096,1,1280]{2,0,1:T(8,128)(2,1)} %fusion.1, bf16[4096,1,1280]{2,0,1:T(8,128)(2,1)} %fusion), kind=kLoop, calls=%fused_computation | loop fusion | flops 10485760 | bytes 41943040 | tf_op jit(solution)/shard_map/stack | solution.py:33
  53.1 147.5 %copy.52 = bf16[4096,2,1280]{2,1,0:T(2,128)(2,1)} copy(bf16[4096,2,1280]{2,0,1:T(8,128)(2,1)S(1)} %pad_maximum_fusion) | data formatting | bytes 41943040 | tf_op jit(solution)/shard_map/stack | solution.py:33
  200.7 42.4 %convert_element_type.60 = bf16[8192,1280]{1,0:T(8,128)(2,1)} reshape(bf16[4096,2,1280]{2,1,0:T(2,128)(2,1)} %copy.52) | data formatting | bytes 41943040 | tf_op jit(solution)/shard_map/convert_element_type | solution.py:47
  243.1 0.0 reduce-scatter.9.cloned.1.call-update
  243.1 0.0 copy-start.6
  243.1 0.0 copy-start.7
  243.1 0.0 copy-start.5
  243.1 0.0 copy-start.3
  243.1 0.0 copy-start.4
  243.2 0.0 all-gather.2.cloned.1.call-start
  243.2 2.4 copy.54
  245.6 2.4 copy.55
  248.0 0.0 copy-done.6
  248.1 0.0 copy-done.7
  248.1 0.0 copy-done.5
  248.1 2.1 convert_multiply_fusion
  250.2 2.7 copy-done.2
  252.9 3.0 multiply_add_fusion.1
  256.0 197.7 %reduce-scatter.9.cloned.1.call-done = bf16[1024,1280]{1,0:T(8,128)(2,1)} async-done(((bf16[8192,1280]{1,0:T(8,128)(2,1)}), bf16[1024,1280]{1,0:T(8,128)(2,1)}) %reduce-scatter.9.cloned.1.call-update) | async-done | bytes 2621456 | tf_op jit(solution)/shard_map/reduce_scatter | solution.py:46
  453.6 7.0 reshape.117
  460.6 16.6 %fusion.12 = (bf16[512,2]{0,1:T(2,128)(2,1)S(1)}, bf16[512,2,1280]{2,0,1:T(8,128)(2,1)S(1)}, f32[512,2,1280]{2,0,1:T(8,128)}) fusion(f32[512,1,1280]{2,0,1:T(8,128)} %get-tuple-element.68, f32[512,1,1280]{2,0,1:T(8,128)} %get-tuple-element.67, f32[512,2]{0,1:T(2,128)S(1)} %pad_maximum_fusion.2, f32[512,2,1280]{2,1,0:T(2,128)} %reshape.117), kind=kLoop, calls=%fused_computation.53 | loop fusion | flops 98302976 | bytes 18356224 | tf_op jit(solution)/shard_map/reduce_sum | solution.py:65
  477.2 4.2 copy.56
  481.4 0.0 all-gather.2.cloned.1.call-update
  481.4 0.0 reduce-scatter.13.cloned.1.call-start
  481.5 0.8 copy.69
  482.3 4.7 multiply_multiply_fusion.5
  487.0 6.2 multiply_reduce_fusion.3
  493.3 0.0 reduce-scatter.13.cloned.1.call-update
  493.3 0.0 reduce-scatter.15.cloned.1.call-start
  493.4 0.2 copy.67
  493.6 0.8 reshape.120
  494.4 0.0 reduce-scatter.15.cloned.1.call-update
  494.4 0.0 reduce-scatter.11.cloned.1.call-start
  494.5 171.0 %all-gather.2.cloned.1.call-done = bf16[4096,2,1280]{2,1,0:T(2,128)(2,1)} async-done(((bf16[512,2,1280]{2,1,0:T(2,128)(2,1)}), bf16[4096,2,1280]{2,1,0:T(2,128)(2,1)}) %all-gather.2.cloned.1.call-update) | async-done | bytes 20971536 | tf_op jit(solution)/shard_map/all_gather | solution.py:66
  665.4 39.8 %fusion.14 = (bf16[4096,1,1280]{2,1,0:T(2,128)(2,1)}, bf16[4096,1,1280]{2,1,0:T(2,128)(2,1)}) fusion(bf16[4096,2,1280]{2,1,0:T(2,128)(2,1)} %all-gather.2.cloned.1.call-done), kind=kLoop, calls=%fused_computation.54 | loop fusion | bytes 41943040 | tf_op jit(solution)/shard_map/slice | solution.py:69
  705.2 0.0 copy-start.9
  705.2 22.9 %fusion.3 = bf16[1,1152,4096]{1,2,0:T(8,128)(2,1)} fusion(bf16[1280,1152]{1,0:T(8,128)(2,1)S(1)} %copy-done, bf16[4096,1,1280]{2,1,0:T(2,128)(2,1)} %get-tuple-element.61), kind=kOutput, calls=%fused_computation.9 | convolution fusion | flops 12084314112 | bytes 22872064 | tf_op jit(solution)/shard_map/dot_general | solution.py:73
  728.1 23.2 %fusion.2 = bf16[1,1152,4096]{1,2,0:T(8,128)(2,1)} fusion(bf16[1280,1152]{1,0:T(8,128)(2,1)S(1)} %copy-done.9, bf16[4096,1,1280]{2,1,0:T(2,128)(2,1)} %get-tuple-element.62), kind=kOutput, calls=%fused_computation.8 | convolution fusion | flops 12084314112 | bytes 22872064 | tf_op jit(solution)/shard_map/dot_general | solution.py:72
  751.3 16.9 %pad_maximum_fusion.1 = bf16[2,1152,4096]{1,2,0:T(8,128)(2,1)} fusion(bf16[1,1152,4096]{1,2,0:T(8,128)(2,1)} %fusion.3, bf16[1,1152,4096]{1,2,0:T(8,128)(2,1)} %fusion.2), kind=kLoop, calls=%fused_computation.1 | loop fusion | flops 9437184 | bytes 37748736 | tf_op jit(solution)/shard_map/stack | solution.py:75
  768.2 0.0 reduce-scatter.11.cloned.1.call-update
  768.2 2.9 fusion.5
  771.1 1.7 slice_bitcast_fusion.2
  772.8 2.6 copy.62
  775.4 2.4 copy.61
  777.8 0.8 copy.66
  778.7 0.5 slice_bitcast_fusion.4
  779.2 0.8 reshape.121
  780.1 0.1 copy.68
  780.2 0.6 convert_element_type.76
  780.8 25.1 %convolution_convert_fusion.4 = bf16[1280,1152]{1,0:T(8,128)(2,1)} fusion(bf16[1152,4096]{1,0:T(8,128)(2,1)} %param.14, bf16[4096,1,1280]{2,1,0:T(2,128)(2,1)} %get-tuple-element.61), kind=kOutput, calls=%fused_computation.13 | convolution fusion | flops 12081070080 | bytes 22872064 | tf_op jit(solution)/shard_map/dot_general | solution.py:71
  805.9 25.2 %convolution_convert_fusion.5 = bf16[1280,1152]{1,0:T(8,128)(2,1)} fusion(bf16[1152,4096]{1,0:T(8,128)(2,1)} %param.13, bf16[4096,1,1280]{2,1,0:T(2,128)(2,1)} %get-tuple-element.62), kind=kOutput, calls=%fused_computation.14 | convolution fusion | flops 12081070080 | bytes 22872064 | tf_op jit(solution)/shard_map/dot_general | solution.py:70
  831.1 106.3 %reduce-scatter.11.cloned.1.call-done = bf16[2,1152,1024]{1,2,0:T(8,128)(2,1)} async-done(((bf16[2,1152,4096]{1,2,0:T(8,128)(2,1)}), bf16[2,1152,1024]{1,2,0:T(8,128)(2,1)}) %reduce-scatter.11.cloned.1.call-update) | async-done | bytes 4718608 | tf_op jit(solution)/shard_map/reduce_scatter | solution.py:77
  937.4 2.9 convert_element_type.71
  940.4 4.3 slice_bitcast_fusion
  944.6 6.2 copy.64
  950.8 6.0 copy.63
  956.9 0.0 copy-done.1
  (12 shorter events, 0.1 us)
Async XLA Ops:
  7.2 19.9 %copy-start = (bf16[1280,1152]{1,0:T(8,128)(2,1)S(1)}, bf16[1280,1152]{1,0:T(8,128)(2,1)}, u32[]{:S(2)}) copy-start(bf16[1280,1152]{1,0:T(8,128)(2,1)} %param.12) | copy-start | bytes 8847364
  7.2 446.4 %reduce-scatter.9.cloned.1.call-start = ((), (), s32[]{:S(2)}) async-start(), calls=%async_computation.4 | async-start | bytes 23592960 | tf_op jit(solution)/shard_map/reduce_scatter | solution.py:46
  7.2 19.8 %copy-start.8 = (bf16[1152,4096]{1,0:T(8,128)(2,1)S(1)}, bf16[1152,4096]{1,0:T(8,128)(2,1)}, u32[]{:S(2)}) copy-start(bf16[1152,4096]{1,0:T(8,128)(2,1)} %param.14) | copy-start | bytes 28311556
  243.1 5.0 copy-start.6
  243.1 5.0 copy-start.7
  243.1 5.0 copy-start.5
  243.1 5.0 copy-start.3
  243.1 5.0 copy-start.4
  243.2 422.3 %all-gather.2.cloned.1.call-start = ((), (), s32[]{:S(2)}) async-start(), calls=%async_computation.5 | async-start | bytes 23592960 | tf_op jit(solution)/shard_map/all_gather | solution.py:66
  250.2 2.7 copy-start.2
  481.4 296.4 %reduce-scatter.13.cloned.1.call-start = ((), (), s32[]{:S(2)}) async-start(), calls=%async_computation.7 | async-start | bytes 163840
  493.3 285.9 %reduce-scatter.15.cloned.1.call-start = ((), (), s32[]{:S(2)}) async-start(), calls=%async_computation.8 | async-start | bytes 163840
  494.4 443.0 %reduce-scatter.11.cloned.1.call-start = ((), (), s32[]{:S(2)}) async-start(), calls=%async_computation.6 | async-start | bytes 23592960 | tf_op jit(solution)/shard_map/reduce_scatter | solution.py:77
  705.2 22.9 %copy-start.9 = (bf16[1280,1152]{1,0:T(8,128)(2,1)S(1)}, bf16[1280,1152]{1,0:T(8,128)(2,1)}, u32[]{:S(2)}) copy-start(bf16[1280,1152]{1,0:T(8,128)(2,1)} %param.11) | copy-start | bytes 8847364
  944.6 12.2 %copy-start.1 = (bf16[1280,1152]{1,0:T(8,128)(2,1)S(1)}, bf16[1280,1152]{1,0:T(8,128)(2,1)}, u32[]{:S(2)}) copy-start(bf16[1280,1152]{1,0:T(8,128)(2,1)} %param.12) | copy-start | bytes 8847364
Sparse Core Ops, SparseCore 0:
  243.2 210.3 reduce-scatter.8
  481.5 183.8 all-gather.1
  668.7 22.0 reduce-scatter.12
  693.6 23.8 reduce-scatter.14
  768.3 169.0 reduce-scatter.10
where the time goes:
time: 979 us; the launch traced here: 964 us
  waiting for transfers between devices  475 us (49%)
  local copies, waits for them, and re-layouts  276 us (28%)
  matrix products  132 us (13%)
  other arithmetic  66.1 us (7%)
  between operations  14.2 us (1%)
    reduce_scatter x1, waiting for transfers between devices, shards(): lax.psum_scatter(partial_term(2 * local_ch * lax.axis_size('feat')).astyp...  198 us
    all_gather x1, waiting for transfers between devices, shards(): piece = lax.all_gather(grad_low, 'feat', axis=0, tiled=True)  171 us
    another operation x1, local copies, waits for them, and re-layouts, partial_term(): return jnp.stack([part_a, part_b], axis=1).reshape(2 * width, rows_here)  148 us
    reduce_scatter x1, waiting for transfers between devices, shards(): lax.psum_scatter(weight_acc.astype(jnp.bfloat16), 'rows', scatter_dimensi...  106 us
    convert_element_type x1, local copies, waits for them, and re-layouts, shards(): partial_term(2 * local_ch * lax.axis_size('feat')).astype(jnp.bfloat16)  42.4 us
    slice x1, local copies, waits for them, and re-layouts, shards(): piece_b = piece[:, 1, :]  39.8 us
    unnamed x32, local copies, waits for them, and re-layouts  28.5 us
    dot_general x1, matrix products, shards(): lax.dot_general(piece_a, weight_a, contract_first, preferred_element_type...  25.2 us
  transfers between devices with their start and end apart: 5, of which 3 were waited for; matrix products, arithmetic and copies ran while one was open for 20% of the time, Pallas kernels for 0%

commit v1 on v0

v1 whole, which is shorter than its diff:
```python
import functools

import jax
import jax.numpy as jnp
from jax import lax
from jax.experimental import pallas as pl
from jax.experimental.pallas import tpu as pltpu
from jax.sharding import PartitionSpec as P

MESH = pl.DeviceIdType.MESH
F32 = jnp.float32
BF16 = jnp.bfloat16
LANE = 128
ROW_BLOCKS = 5
SUBS = 2
RIGHT, LEFT = 0, 1
FAR, NEAR, KEEP, OWN = 0, 1, 2, 3
INV_SQRT2 = 0.7071067811865476
INV_SQRT_2PI = 0.3989422804014327


def dot(lhs, rhs):
    return lax.dot_general(lhs, rhs, (((1,), (0,)), ((), ())), preferred_element_type=F32)


def dot_t(lhs, rhs):
    return lax.dot_general(lhs, rhs, (((1,), (1,)), ((), ())), preferred_element_type=F32)


def kernel(line, rows, width, chl, *refs):
    (
        pool_a, pool_b, weight_a, weight_b, par, scale, og_a, og_b,
        mixed_a, mixed_b, pg_a, pg_b, wg_a, wg_b, stats,
        pool_v, pool_t, wf, wb, part, xr, rbuf, gath, acc, wsend, wrecv, wout,
        og_v, mix_v, pg_v, sacc, sred, srecv,
        pool_s, wf_s, wb_s, xs_send, xs_recv, z_send, z_recv, g_send, g_recv,
        w_send, w_recv, wout_s, og_s, mix_s, pg_s, st_send, st_recv, credit, wcredit,
    ) = refs
    L = line
    NB, NS = ROW_BLOCKS, SUBS
    RB = rows // NB
    SB = RB // NS
    NCH = chl // LANE
    U = NCH * NB
    HALF = L // 2
    SENDING = U + 2
    TICKS = (U + 2 + NB) * L
    pools, weights = (pool_a, pool_b), (weight_a, weight_b)
    ogs, mixeds = (og_a, og_b), (mixed_a, mixed_b)
    pgs, wgs = (pg_a, pg_b), (wg_a, wg_b)

    f = lax.axis_index("feat")
    r = lax.axis_index("rows")
    p = lax.div(f, 2)
    c = lax.rem(f, 2)
    sib = f + 1 - 2 * c
    xp = r + 1 - 2 * lax.rem(r, 2)
    yp = lax.rem(r + 2, 4)
    dp = 3 - r
    has_left, has_right = p > 0, p < L - 1
    pos = (p, L - 1 - p)
    nxt = (f + 2, f - 2)

    def remote(src, dst, send, recv, **dev):
        return pltpu.make_async_remote_copy(
            src_ref=src, dst_ref=dst, send_sem=send, recv_sem=recv, device_id=dev, device_id_type=MESH
        )

    def signal(sem, **dev):
        pl.semaphore_signal(sem, inc=1, device_id=dev, device_id_type=MESH)

    def lanes(index):
        return pl.ds(pl.multiple_of(index * LANE, LANE), LANE)

    def block_rows(i):
        return pl.ds(pl.multiple_of(i * RB, RB), RB)

    def sub_rows(b):
        return pl.ds(b * SB, SB)

    def pool_load(u, t):
        slot = lax.rem(u, 2)
        return pltpu.make_async_copy(
            pools[t].at[block_rows(lax.rem(u, NB)), :], pool_v.at[slot, t], pool_s.at[slot, t]
        )

    def wf_loads(tick):
        j = lax.div(tick, L * NB)
        s = lax.rem(tick, L)
        slot = lax.rem(tick, 2)
        core = jnp.where(s < HALF, 1 - c, c)
        first = 2 * lax.rem(s, HALF)
        out = []
        for t in range(2):
            for k in range(2):
                owner = 2 * (first + k) + core
                out.append(
                    pltpu.make_async_copy(
                        weights[t].at[:, lanes(owner * NCH + j)],
                        wf.at[slot, t, :, k * LANE : (k + 1) * LANE],
                        wf_s.at[slot, t, k],
                    )
                )
        return out

    def wb_loads(j, t):
        out = []
        for q in range(L):
            for k in range(2):
                out.append(
                    pltpu.make_async_copy(
                        weights[t].at[:, lanes((2 * q + k) * NCH + j)],
                        wb.at[t, q, :, k * LANE : (k + 1) * LANE],
                        wb_s.at[t, q, k],
                    )
                )
        return out

    def og_load(u, t):
        slot = lax.rem(u, 2)
        return pltpu.make_async_copy(
            ogs[t].at[block_rows(lax.rem(u, NB)), lanes(lax.div(u, NB))], og_v.at[slot, t], og_s.at[slot, t]
        )

    def mix_store(u, b, t):
        i, j = lax.rem(u, NB), lax.div(u, NB)
        dst = pl.ds(pl.multiple_of(i * RB + b * SB, SB), SB)
        return pltpu.make_async_copy(mix_v.at[b, t], mixeds[t].at[dst, lanes(j)], mix_s.at[b, t])

    def part_copy(u, tile, per3):
        return remote(
            part.at[lax.rem(u, 2), 0, pl.ds(2 * tile, 2)],
            xr.at[lax.rem(u, 4), pl.ds(2 * tile, 2)],
            xs_send.at[tile],
            xs_recv.at[tile, per3],
            feat=sib,
        )

    def gath_block(u, o, b):
        i, j = lax.rem(u, NB), lax.div(u, NB)
        return gath.at[lax.rem(j, 2), o, c, pl.ds(pl.multiple_of(i * RB + b * SB, SB), SB), :]

    def gath_copy(u, o, d, b, s, per3):
        block = gath_block(u, o, b)
        return remote(block, block, z_send.at[d, b, s], z_recv.at[d, b, s, per3], feat=nxt[d])

    def share_copy(u, o, d, b, s, per3):
        block = gath_block(u, o, b)
        return remote(block, block, g_send.at[d, b, s], g_recv.at[d, b, s, per3], feat=sib)

    def share_wait(u, o, d, b, s, per3):
        i, j = lax.rem(u, NB), lax.div(u, NB)
        block = gath.at[lax.rem(j, 2), o, 1 - c, pl.ds(pl.multiple_of(i * RB + b * SB, SB), SB), :]
        remote(block, block, g_send.at[d, b, s], g_recv.at[d, b, s, per3], feat=sib).wait_recv()

    def sum_copy(u, d, b, s, per3):
        u3 = lax.rem(u, 3)
        return remote(
            rbuf.at[u3, d, s - 1, sub_rows(b), :],
            rbuf.at[u3, d, s, sub_rows(b), :],
            z_send.at[d, b, s],
            z_recv.at[d, b, s, per3],
            feat=nxt[d],
        )

    def sum_wait(u, d, b, s, per3):
        u3 = lax.rem(u, 3)
        block = rbuf.at[u3, d, s, sub_rows(b), :]
        remote(block, block, z_send.at[d, b, s], z_recv.at[d, b, s, per3], feat=nxt[d]).wait_recv()

    def own_sum(u, o, b):
        mine = part[lax.rem(u, 2), 1, o, sub_rows(b), :].astype(F32)
        return mine + xr[lax.rem(u, 4), o, sub_rows(b), :].astype(F32)

    def fold(v):
        return jnp.sum(v.reshape(SB // 8, 8, LANE), axis=0)

    def finalize(u, b, per):
        i, j = lax.rem(u, NB), lax.div(u, NB)
        last3 = lax.rem(per - 1, 3)

        @pl.when(has_left)
        def _():
            sum_wait(u, RIGHT, b, L - 1, last3)

        @pl.when(has_right)
        def _():
            sum_wait(u, LEFT, b, L - 1, last3)

        if b == 0:
            og_load(u, 0).wait()
            og_load(u, 1).wait()

        @pl.when(u >= 1)
        def _():
            mix_store(u, b, 0).wait()
            mix_store(u, b, 1).wait()

        u3 = lax.rem(u, 3)
        total = own_sum(u, p, b)
        total = total + rbuf[u3, RIGHT, L - 1, sub_rows(b), :].astype(F32)
        total = total + rbuf[u3, LEFT, L - 1, sub_rows(b), :].astype(F32)
        ch = lanes(j)
        s00, s01, s10, s11 = (par[k : k + 1, ch] for k in range(4))
        here = pl.ds(pl.multiple_of(i * RB + b * SB, SB), SB)
        row = scale[here, :]
        gy_a = row * og_v[lax.rem(u, 2), 0, sub_rows(b), :].astype(F32)
        gy_b = row * og_v[lax.rem(u, 2), 1, sub_rows(b), :].astype(F32)

        def gelu(v):
            cdf = 0.5 * (1.0 + lax.erf(v * INV_SQRT2))
            return v * cdf, cdf + v * (INV_SQRT_2PI * jnp.exp(-0.5 * v * v))

        act_a, slope_a = gelu(total[:, :LANE] + par[4:5, ch])
        act_b, slope_b = gelu(total[:, LANE:] + par[5:6, ch])
        mix_v[b, 0] = (row * (s00 * act_a + s01 * act_b)).astype(BF16)
        mix_v[b, 1] = (row * (s10 * act_a + s11 * act_b)).astype(BF16)
        mix_store(u, b, 0).start()
        mix_store(u, b, 1).start()
        gpre_a = ((s00 * gy_a + s10 * gy_b) * slope_a).astype(BF16)
        gpre_b = ((s01 * gy_a + s11 * gy_b) * slope_b).astype(BF16)
        gath[lax.rem(j, 2), p, c, here, :LANE] = gpre_a
        gath[lax.rem(j, 2), p, c, here, LANE:] = gpre_b
        sacc[j, 0] += fold(gy_a * act_a)
        sacc[j, 1] += fold(gy_a * act_b)
        sacc[j, 2] += fold(gy_b * act_a)
        sacc[j, 3] += fold(gy_b * act_b)
        sacc[j, 4] += fold(gpre_a.astype(F32))
        sacc[j, 5] += fold(gpre_b.astype(F32))

    def first_partner(t):
        return jnp.where(t == 0, xp, yp)

    def second_partner(t):
        return jnp.where(t == 0, yp, xp)

    def w_copy(t, kind):
        dst = KEEP if kind == KEEP else kind
        return remote(
            wsend.at[t, kind],
            wrecv.at[t, dst],
            w_send.at[t, kind],
            w_recv.at[t, dst],
            rows=second_partner(t) if kind == KEEP else first_partner(t),
        )

    per_row = 2 * L // 4

    def wout_stores(j, t):
        return [
            pltpu.make_async_copy(
                wout.at[t, :, k * LANE : (k + 1) * LANE], wgs[t].at[:, lanes(k * NCH + j)], wout_s.at[t, k]
            )
            for k in range(per_row)
        ]

    def pg_store(t, i, slot):
        return pltpu.make_async_copy(pg_v.at[slot], pgs[t].at[block_rows(i), :], pg_s.at[slot])

    for t in range(2):
        pool_load(0, t).start()
    for copy in wf_loads(0):
        copy.start()

    bar = pltpu.get_barrier_semaphore()

    @pl.when(has_left)
    def _():
        signal(bar, feat=f - 2)

    @pl.when(has_right)
    def _():
        signal(bar, feat=f + 2)

    signal(bar, feat=sib)
    signal(bar, rows=xp)
    signal(bar, rows=yp)
    signal(bar, rows=dp)
    sacc[...] = jnp.zeros_like(sacc)

    @pl.when(jnp.logical_not(has_left))
    def _():
        for k in range(3):
            rbuf[k, RIGHT, L - 1] = jnp.zeros((RB, 2 * LANE), BF16)

    @pl.when(jnp.logical_not(has_right))
    def _():
        for k in range(3):
            rbuf[k, LEFT, L - 1] = jnp.zeros((RB, 2 * LANE), BF16)

    pl.semaphore_wait(bar, 4 + has_left.astype(jnp.int32) + has_right.astype(jnp.int32))

    def tick(T, carry):
        per, s = lax.div(T, L), lax.rem(T, L)
        per3 = lax.rem(per, 3)
        u = per - 2
        ur = per - 1
        uf = per
        gathers = (u >= 0) & (u < U)
        gathered = (u >= 1) & (u <= U)
        sums = (ur >= 0) & (ur < U)
        summed = (ur >= 1) & (ur <= U)

        @pl.when((s == 0) & (per >= 2) & (per < SENDING))
        def _():
            @pl.when(has_left)
            def _():
                pl.semaphore_wait(credit.at[0], 1)

            @pl.when(has_right)
            def _():
                pl.semaphore_wait(credit.at[1], 1)

            pl.semaphore_wait(credit.at[2], 1)

        @pl.when((s == 1) & sums)
        def _():
            for k in range(HALF):
                part_copy(ur, k, lax.rem(per - 1, 3)).wait_recv()

        for b in range(NS):

            @pl.when((s == 0) & gathers)
            def _():
                finalize(u, b, per)

            for d in (RIGHT, LEFT):
                gather_here = pos[d] >= s
                o = p - s if d == RIGHT else p + s
                dest = p + (L - s) if d == RIGHT else p - (L - s)
                shares = (s >= 1) if d == LEFT else (s >= 0)

                @pl.when(gathered & gather_here)
                def _():
                    @pl.when(pos[d] < L - 1)
                    def _():
                        gath_copy(u, o, d, b, s, per3).wait_send()

                    @pl.when(shares)
                    def _():
                        share_copy(u, o, d, b, s, per3).wait_send()

                @pl.when(gathers & gather_here)
                def _():
                    @pl.when(s >= 1)
                    def _():
                        gath_copy(u, o, d, b, s - 1, per3).wait_recv()

                    @pl.when(pos[d] < L - 1)
                    def _():
                        gath_copy(u, o, d, b, s, per3).start()

                    @pl.when(shares)
                    def _():
                        share_copy(u, o, d, b, s, per3).start()

                @pl.when(summed & jnp.logical_not(gather_here))
                def _():
                    sum_copy(ur, d, b, s, per3).wait_send()

                @pl.when(sums & jnp.logical_not(gather_here))
                def _():
                    u3 = lax.rem(ur, 3)

                    @pl.when(pos[d] >= 1)
                    def _():
                        sum_wait(ur, d, b, s - 1, per3)
                        both = own_sum(ur, dest, b) + rbuf[u3, d, s - 1, sub_rows(b), :].astype(F32)
                        rbuf[u3, d, s - 1, sub_rows(b), :] = both.astype(BF16)

                    @pl.when(pos[d] < 1)
                    def _():
                        rbuf[u3, d, s - 1, sub_rows(b), :] = own_sum(ur, dest, b).astype(BF16)

                    sum_copy(ur, d, b, s, per3).start()

        before = T - 1 + L
        per_m, s_m = lax.div(before, L) - 1, lax.rem(before, L)
        u_m = per_m - 2

        @pl.when((u_m >= 0) & (u_m < U))
        def _():
            for b in range(NS):
                for d in (RIGHT, LEFT):
                    o = p - s_m if d == RIGHT else p + s_m
                    shares = (s_m >= 1) if d == LEFT else (s_m >= 0)

                    @pl.when((pos[d] >= s_m) & shares)
                    def _():
                        share_wait(u_m, o, d, b, s_m, lax.rem(per_m, 3))

        @pl.when((s == 1) & (ur >= 0) & (ur < U))
        def _():
            og_load(ur, 0).start()
            og_load(ur, 1).start()

        @pl.when((uf >= 1) & (uf <= U) & (s < HALF))
        def _():
            part_copy(uf, s, per3).wait_send()

        @pl.when(uf < U)
        def _():
            u2 = lax.rem(uf, 2)

            @pl.when(s == 0)
            def _():
                for t in range(2):
                    pool_load(uf, t).wait()

                @pl.when(uf + 1 < U)
                def _():
                    for t in range(2):
                        pool_load(uf + 1, t).start()

            for copy in wf_loads(T):
                copy.wait()

            @pl.when(T + 1 < U * L)
            def _():
                for copy in wf_loads(T + 1):
                    copy.start()

            which = lax.div(s, HALF)
            first = 2 * lax.rem(s, HALF)
            for t in range(2):
                res = dot(pool_v[u2, t], wf[lax.rem(T, 2), t]).astype(BF16)
                part[u2, which, first, :, t * LANE : (t + 1) * LANE] = res[:, :LANE]
                part[u2, which, first + 1, :, t * LANE : (t + 1) * LANE] = res[:, LANE:]

            @pl.when(s < HALF)
            def _():
                part_copy(uf, s, per3).start()

            @pl.when((uf < NB) & (s == L - 1))
            def _():
                for t in range(2):
                    pool_t[t, :, block_rows(uf)] = pool_v[u2, t].T

        since = jnp.maximum(T - 2 * L, 0)
        jb = lax.div(since, NB * L) - 1
        tau = lax.rem(since, NB * L)
        jb2 = lax.rem(jb, 2)

        @pl.when(jb >= 0)
        def _():
            @pl.when((tau == 0) & (jb >= 1))
            def _():
                pl.semaphore_wait(wcredit.at[0], 1)

            @pl.when((tau == 1) & (jb >= 1))
            def _():
                pl.semaphore_wait(wcredit.at[1], 1)

            for t in range(2):

                @pl.when(tau == 2 + t)
                def _():
                    for copy in wb_loads(jb, t):
                        copy.start()

            @pl.when(tau < 8)
            def _():
                t = lax.rem(tau, 2)
                kind = lax.div(tau, 2)
                one, two = first_partner(t), second_partner(t)
                owner = jnp.where(kind == FAR, dp, jnp.where(kind == NEAR, one, jnp.where(kind == KEEP, two, r)))
                cols = []
                for k in range(per_row):
                    fo = owner * per_row + k
                    cols.append(gath[jb2, lax.div(fo, 2), lax.rem(fo, 2), :, lanes(t)])
                cols = jnp.concatenate(cols, axis=1)
                step = 384 if width % 384 == 0 else LANE
                for m in range(0, width, step):
                    wsend[t, kind, m : m + step, :] = dot(pool_t[t, m : m + step, :], cols).astype(BF16)
                for way in (FAR, NEAR):

                    @pl.when(kind == way)
                    def _():
                        w_copy(t, way).start()

            for t in range(2):

                @pl.when(tau == 9 + t)
                def _():
                    w_copy(t, FAR).wait_recv()
                    both = wsend[t, KEEP].astype(F32) + wrecv[t, FAR].astype(F32)
                    wsend[t, KEEP] = both.astype(BF16)
                    w_copy(t, KEEP).start()

                @pl.when(tau == 15 + t)
                def _():
                    w_copy(t, NEAR).wait_recv()
                    w_copy(t, KEEP).wait_recv()
                    for kind in (FAR, NEAR, KEEP):
                        w_copy(t, kind).wait_send()

                    @pl.when(jb >= 1)
                    def _():
                        for copy in wout_stores(jb, t):
                            copy.wait()

                    both = wsend[t, OWN].astype(F32) + wrecv[t, NEAR].astype(F32)
                    wout[t] = both + wrecv[t, KEEP].astype(F32)
                    for copy in wout_stores(jb, t):
                        copy.start()

            @pl.when((tau == 17) & (jb < NCH - 1))
            def _():
                signal(wcredit.at[0], rows=xp)
                signal(wcredit.at[1], rows=yp)

            @pl.when((tau >= 8) & (tau < 8 + 2 * NB))
            def _():
                piece = tau - 8
                t = lax.div(piece, NB)
                i = lax.rem(piece, NB)
                for tt in range(2):

                    @pl.when(piece == tt * NB)
                    def _():
                        for copy in wb_loads(jb, tt):
                            copy.wait()

                total = None
                for q in range(L):
                    cols = [gath[jb2, q, k, block_rows(i), lanes(t)] for k in range(2)]
                    term = dot_t(jnp.concatenate(cols, axis=1), wb[t, q])
                    total = term if total is None else total + term

                @pl.when(jb == 0)
                def _():
                    acc[t, block_rows(i), :] = total

                @pl.when((jb > 0) & (jb < NCH - 1))
                def _():
                    acc[t, block_rows(i), :] += total

                @pl.when(jb == NCH - 1)
                def _():
                    slot = lax.rem(piece, 2)

                    @pl.when(piece >= 2)
                    def _():
                        pg_store(0, 0, slot).wait()

                    pg_v[slot] = (acc[t, block_rows(i), :] + total).astype(BF16)
                    for tt in range(2):

                        @pl.when(t == tt)
                        def _():
                            pg_store(tt, i, slot).start()

        @pl.when((s == L - 1) & (per < SENDING - 2))
        def _():
            @pl.when(has_left)
            def _():
                signal(credit.at[1], feat=f - 2)

            @pl.when(has_right)
            def _():
                signal(credit.at[0], feat=f + 2)

            signal(credit.at[2], feat=sib)

        @pl.when(T == (U + 1) * L + 1)
        def _():
            for j in range(NCH):
                for k in range(6):
                    sred[j, k : k + 1, :] = jnp.sum(sacc[j, k], axis=0, keepdims=True)
                sred[j, 6:8, :] = jnp.zeros((2, LANE), F32)
            for k, peer in enumerate((xp, yp, dp)):
                remote(sred.at[peer], srecv.at[k], st_send.at[k], st_recv.at[k], rows=peer).start()

        return carry

    lax.fori_loop(0, TICKS, tick, 0)

    for k, peer in enumerate((xp, yp, dp)):
        copy = remote(sred.at[peer], srecv.at[k], st_send.at[k], st_recv.at[k], rows=peer)
        copy.wait_send()
        copy.wait_recv()
    stats[...] = sred[r] + srecv[0] + srecv[1] + srecv[2]
    for t in range(2):
        for b in range(NS):
            mix_store(U - 1, b, t).wait()
        for copy in wout_stores(NCH - 1, t):
            copy.wait()
        pg_store(0, 0, t).wait()


def fused(line, pool_a, pool_b, weight_a, weight_b, bias_a, bias_b, stitch, row_scale, outgrad_a, outgrad_b):
    rows, width = pool_a.shape
    chl = bias_a.shape[0]
    NB, NS, L = ROW_BLOCKS, SUBS, line
    RB = rows // NB
    SB = RB // NS
    NCH = chl // LANE
    per_row = 2 * L // 4
    par = jnp.concatenate([stitch.reshape(4, chl), bias_a[None], bias_b[None], jnp.zeros((2, chl), F32)], axis=0)
    hbm = pl.BlockSpec(memory_space=pl.ANY)
    vmem = pl.BlockSpec(memory_space=pltpu.VMEM)
    dma = pltpu.SemaphoreType.DMA
    out_shape = (
        jax.ShapeDtypeStruct((rows, chl), BF16),
        jax.ShapeDtypeStruct((rows, chl), BF16),
        jax.ShapeDtypeStruct((rows, width), BF16),
        jax.ShapeDtypeStruct((rows, width), BF16),
        jax.ShapeDtypeStruct((width, per_row * chl), F32),
        jax.ShapeDtypeStruct((width, per_row * chl), F32),
        jax.ShapeDtypeStruct((8, LANE), F32),
    )
    scratch = [
        pltpu.VMEM((2, 2, RB, width), BF16),
        pltpu.VMEM((2, width, rows), BF16),
        pltpu.VMEM((2, 2, width, 2 * LANE), BF16),
        pltpu.VMEM((2, L, width, 2 * LANE), BF16),
        pltpu.VMEM((2, 2, L, RB, 2 * LANE), BF16),
        pltpu.VMEM((4, L, RB, 2 * LANE), BF16),
        pltpu.VMEM((3, 2, L, RB, 2 * LANE), BF16),
        pltpu.VMEM((2, L, 2, rows, 2 * LANE), BF16),
        pltpu.VMEM((2, rows, width), F32),
        pltpu.VMEM((2, 4, width, per_row * LANE), BF16),
        pltpu.VMEM((2, 3, width, per_row * LANE), BF16),
        pltpu.VMEM((2, width, per_row * LANE), F32),
        pltpu.VMEM((2, 2, RB, LANE), BF16),
        pltpu.VMEM((NS, 2, SB, LANE), BF16),
        pltpu.VMEM((2, RB, width), BF16),
        pltpu.VMEM((NCH, 6, 8, LANE), F32),
        pltpu.VMEM((NCH, 8, LANE), F32),
        pltpu.VMEM((3, 8, LANE), F32),
        dma((2, 2)),
        dma((2, 2, 2)),
        dma((2, L, 2)),
        dma((L // 2,)),
        dma((L // 2, 3)),
        dma((2, NS, L)),
        dma((2, NS, L, 3)),
        dma((2, NS, L)),
        dma((2, NS, L, 3)),
        dma((2, 3)),
        dma((2, 3)),
        dma((2, per_row)),
        dma((2, 2)),
        dma((NS, 2)),
        dma((2,)),
        dma((3,)),
        dma((3,)),
        pltpu.SemaphoreType.REGULAR((3,)),
        pltpu.SemaphoreType.REGULAR((2,)),
    ]
    mixed_a, mixed_b, pg_a, pg_b, wg_a, wg_b, stats = pl.pallas_call(
        functools.partial(kernel, line, rows, width, chl),
        out_shape=out_shape,
        in_specs=[hbm, hbm, hbm, hbm, vmem, vmem, hbm, hbm],
        out_specs=(hbm, hbm, hbm, hbm, hbm, hbm, vmem),
        scratch_shapes=scratch,
        compiler_params=pltpu.CompilerParams(
            collective_id=0, has_side_effects=True, vmem_limit_bytes=VMEM_LIMIT
        ),
    )(pool_a, pool_b, weight_a, weight_b, par, row_scale[:, None], outgrad_a, outgrad_b)
    return mixed_a, mixed_b, pg_a, pg_b, wg_a, wg_b, stats[4], stats[5], stats[:4].reshape(2, 2, LANE)


VMEM_LIMIT = 62 * 1024 * 1024


def plain(pool_a, pool_b, weight_a, weight_b, bias_a, bias_b, stitch, row_scale, outgrad_a, outgrad_b):
    row = row_scale[:, None]

    def pre(pool, weight, bias):
        partial = dot(pool, weight).astype(BF16)
        return lax.psum_scatter(partial, "feat", scatter_dimension=1, tiled=True).astype(F32) + bias

    def gelu(v):
        cdf = 0.5 * (1.0 + lax.erf(v * INV_SQRT2))
        return v * cdf, cdf + v * (INV_SQRT_2PI * jnp.exp(-0.5 * v * v))

    act_a, slope_a = gelu(pre(pool_a, weight_a, bias_a))
    act_b, slope_b = gelu(pre(pool_b, weight_b, bias_b))
    (s00, s01), (s10, s11) = stitch[0], stitch[1]
    mixed_a = (row * (s00 * act_a + s01 * act_b)).astype(BF16)
    mixed_b = (row * (s10 * act_a + s11 * act_b)).astype(BF16)
    gy_a = row * outgrad_a.astype(F32)
    gy_b = row * outgrad_b.astype(F32)
    gpre_a = ((s00 * gy_a + s10 * gy_b) * slope_a).astype(BF16)
    gpre_b = ((s01 * gy_a + s11 * gy_b) * slope_b).astype(BF16)
    sums = jnp.stack(
        [
            jnp.sum(v, axis=0)
            for v in (
                gy_a * act_a,
                gy_a * act_b,
                gy_b * act_a,
                gy_b * act_b,
                gpre_a.astype(F32),
                gpre_b.astype(F32),
            )
        ]
    )
    sums = lax.psum_scatter(sums, "rows", scatter_dimension=1, tiled=True)

    def back(pool, weight, gpre):
        whole = lax.all_gather(gpre, "feat", axis=1, tiled=True)
        pool_grad = dot_t(whole, weight).astype(BF16)
        wgrad = lax.dot_general(pool, whole, (((0,), (0,)), ((), ())), preferred_element_type=F32)
        wgrad = lax.psum_scatter(wgrad.astype(BF16), "rows", scatter_dimension=1, tiled=True)
        return pool_grad, wgrad.astype(F32)

    pg_a, wg_a = back(pool_a, weight_a, gpre_a)
    pg_b, wg_b = back(pool_b, weight_b, gpre_b)
    return mixed_a, mixed_b, pg_a, pg_b, wg_a, wg_b, sums[4], sums[5], sums[:4].reshape(2, 2, -1)


def shards(
    pool_a, pool_b, weight_a, weight_b, bias_a, bias_b, stitch, crop_count, row_mask, outgrad_a, outgrad_b
):
    row_scale = row_mask.astype(F32) / crop_count.astype(F32)
    rows, width = pool_a.shape
    chl = bias_a.shape[0]
    n_rows, n_feat = lax.axis_size("rows"), lax.axis_size("feat")
    fits = (
        n_rows == 4
        and n_feat == 8
        and chl == n_rows * LANE
        and width % LANE == 0
        and rows % (ROW_BLOCKS * LANE) == 0
    )
    run = functools.partial(fused, n_feat // 2) if fits else plain
    return run(pool_a, pool_b, weight_a, weight_b, bias_a, bias_b, stitch, row_scale, outgrad_a, outgrad_b)


def solution(mesh):
    return jax.shard_map(
        shards,
        mesh=mesh,
        in_specs=(
            P("rows", "feat"),
            P("rows", "feat"),
            P("feat", None),
            P("feat", None),
            P("feat"),
            P("feat"),
            P(None, None, "feat"),
            P("rows"),
            P("rows"),
            P("rows", "feat"),
            P("rows", "feat"),
        ),
        out_specs=(
            P("rows", "feat"),
            P("rows", "feat"),
            P("rows", "feat"),
            P("rows", "feat"),
            P("feat", "rows"),
            P("feat", "rows"),
            P(("feat", "rows")),
            P(("feat", "rows")),
            P(None, None, ("feat", "rows")),
        ),
        check_vma=False,
    )
```

time: 979 us -> 394 us (0.40); the launches traced: 964 us -> 394 us
  waiting for transfers between devices: 475 us -> 0 us
  Pallas kernels: 0 us -> 371 us
  local copies, waits for them, and re-layouts: 276 us -> 19.8 us
  matrix products: 132 us -> 0 us
  other arithmetic: 66.1 us -> 2.1 us
  between operations: 14.2 us -> 0.68 us
    pallas_call x0 -> x1, Pallas kernels: none -> 371 us  [fused(): pl.pallas_call(functools.partial(kernel, line, rows, width, chl), out_sha...]
    reduce_scatter x2 -> x0, waiting for transfers between devices: 304 us -> none  [the longest x1 198 us: shards(): lax.psum_scatter(partial_term(2 * local_ch * lax.axis_size('feat')).astyp...]
    all_gather x1 -> x0, waiting for transfers between devices: 171 us -> none  [shards(): piece = lax.all_gather(grad_low, 'feat', axis=0, tiled=True)]
    another operation x1 -> x0, local copies, waits for them, and re-layouts: 148 us -> none  [partial_term(): return jnp.stack([part_a, part_b], axis=1).reshape(2 * width, rows_here)]
    dot_general x6 -> x0, matrix products: 132 us -> none  [the longest x1 25.2 us: shards(): lax.dot_general(piece_a, weight_a, contract_first, preferred_element_type...]
    convert_element_type x3 -> x0, local copies, waits for them, and re-layouts: 48.3 us -> none  [the longest x1 42.4 us: shards(): partial_term(2 * local_ch * lax.axis_size('feat')).astype(jnp.bfloat16)]
    slice x2 -> x1, local copies, waits for them, and re-layouts: 39.8 us -> 1.26 us  [fused(): stats[:4].reshape(2, 2, LANE)]
    another operation x4 -> x0, other arithmetic: 29.8 us -> none  [the longest x1 16.9 us: shards(): weight_acc = jnp.stack([wgrad_a, wgrad_b], axis=0)]
  transfers between devices with their start and end apart: 5 -> 0, of which waited for: 3 -> 0; matrix products, arithmetic and copies ran while one was open for 20% -> 0% of each run, Pallas kernels for 0% -> 0%
where the time goes in v1:
time: 394 us
  Pallas kernels  371 us (94%)
  local copies, waits for them, and re-layouts  19.8 us (5%)
    pallas_call x1, Pallas kernels, fused(): pl.pallas_call(functools.partial(kernel, line, rows, width, chl), out_sha...  371 us
    unnamed x18, local copies, waits for them, and re-layouts  15.3 us

profile of v1, /device:TPU:0, one launch (start us, length us, event | category | flops | bytes accessed | tf_op | source)
XLA Modules:
  0.0 393.7 jit_solution(13703453109635510171)
XLA Ops:
  0.7 0.1 pad.3.clone
  0.7 0.7 reshape.24
  1.4 1.4 maximum_maximum_fusion.refs_4_
  2.8 0.7 convert_divide_fusion
  3.5 1.1 broadcast_in_dim.16.refs_5_
  4.6 371.1 %shard_map.178 = (bf16[1280,512]{1,0:T(8,128)(2,1)}, bf16[1280,512]{1,0:T(8,128)(2,1)}, bf16[1280,1152]{1,0:T(8,128)(2,1)}, bf16[1280,1152]{1,0:T(8,128)(2,1)}, ...) custom-call(bf16[1280,1152]{1,0:T(8,128)(2,1)} %refs_0_.1, bf16[1280,1152]{1,0:T(8,128)(2,1)} %refs_1_.1, ...), custom_call_target="tpu_custom_call" | custom-call | tf_op jit(solution)/shard_map/pallas_call | solution.py:651
  375.7 0.0 copy-start.1
  375.7 1.4 slice_bitcast_fusion
  377.1 1.3 slice.11
  378.4 2.5 copy.27
  380.8 0.0 slice-start.2
  380.8 2.6 copy.28
  383.4 0.0 copy-done.1
  383.4 0.0 copy-start
  383.4 0.0 slice-start.3
  383.4 1.6 copy.29
  385.0 1.3 copy-done
  386.3 0.0 slice-start
  386.3 1.6 copy.30
  387.9 0.0 slice-done.2
  387.9 0.0 slice-done.3
  387.9 0.0 slice-start.1
  387.9 2.4 copy.31
  390.3 1.0 slice-done
  391.3 0.2 slice-done.1
  391.5 2.2 copy.32
  (3 shorter events, 0.0 us)
Async XLA Ops:
  375.7 7.7 %copy-start.1 = (bf16[1280,1152]{1,0:T(8,128)(2,1)S(1)}, bf16[1280,1152]{1,0:T(8,128)(2,1)}, u32[]{:S(2)}) copy-start(bf16[1280,1152]{1,0:T(8,128)(2,1)} %get-tuple-element.36) | copy-start | bytes 8847364
  380.8 7.1 %slice-start.2 = ((s8[4718592]{0:T(1024)(128)(4,1)}), s8[4194304]{0:T(1024)(128)(4,1)S(1)}, s32[]{:S(2)}) async-start(s8[4718592]{0:T(1024)(128)(4,1)} %bitcast.9), calls=%async_computation.2 | async-start | bytes 8388608
  383.4 2.9 copy-start
  383.4 4.5 %slice-start.3 = ((s8[4718592]{0:T(1024)(128)(4,1)}), s8[524288]{0:T(1024)(128)(4,1)S(1)}, s32[]{:S(2)}) async-start(s8[4718592]{0:T(1024)(128)(4,1)} %bitcast.9), calls=%async_computation.3 | async-start | bytes 1048576
  386.3 5.0 %slice-start = ((s8[4718592]{0:T(1024)(128)(4,1)}), s8[4194304]{0:T(1024)(128)(4,1)S(1)}, s32[]{:S(2)}) async-start(s8[4718592]{0:T(1024)(128)(4,1)} %bitcast.7), calls=%async_computation | async-start | bytes 8388608
  387.9 3.6 slice-start.1

commit v2 on v1

v2 whole, which is shorter than its diff:
```python
import functools

import jax
import jax.numpy as jnp
from jax import lax
from jax.experimental import pallas as pl
from jax.experimental.pallas import tpu as pltpu
from jax.sharding import PartitionSpec as P

MESH = pl.DeviceIdType.MESH
F32 = jnp.float32
BF16 = jnp.bfloat16
LANE = 128
ROW_BLOCKS = 2
SUBS = 5
PIECES = 4
RIGHT, LEFT = 0, 1
FAR, NEAR, KEEP, OWN = 0, 1, 2, 3
SIB, MINE = 0, 1
INV_SQRT2 = 0.7071067811865476
INV_SQRT_2PI = 0.3989422804014327


def dot(lhs, rhs):
    return lax.dot_general(lhs, rhs, (((1,), (0,)), ((), ())), preferred_element_type=F32)


def dot_t(lhs, rhs):
    return lax.dot_general(lhs, rhs, (((1,), (1,)), ((), ())), preferred_element_type=F32)


def kernel(rows, width, chl, *refs):
    (
        pool_a, pool_b, weight_a, weight_b, par, scale, og_a, og_b,
        mixed_a, mixed_b, pg_a, pg_b, wg_a, wg_b, stats,
        pool_v, pool_t, wf, wb, part_sib, part_own, xr, rbuf, gath, acc, wsend, wrecv, wout,
        og_v, mix_v, pg_v, sacc, sred, srecv,
        pool_s, wf_s, wb_s, xs_send, xs_recv, z_send, z_recv, g_send, g_recv,
        w_send, w_recv, wout_s, og_s, mix_s, pg_s, st_send, st_recv, credit, wcredit,
    ) = refs
    L = 4
    NB, NS = ROW_BLOCKS, SUBS
    RB = rows // NB
    SB = RB // NS
    PB = rows // PIECES
    NCH = chl // LANE
    U = NCH * NB
    SENDING = U + 2
    TICKS = (U + 2 + NB) * L
    pools, weights = (pool_a, pool_b), (weight_a, weight_b)
    ogs, mixeds = (og_a, og_b), (mixed_a, mixed_b)
    pgs, wgs = (pg_a, pg_b), (wg_a, wg_b)

    f = lax.axis_index("feat")
    r = lax.axis_index("rows")
    p = lax.div(f, 2)
    c = lax.rem(f, 2)
    sib = f + 1 - 2 * c
    xp = r + 1 - 2 * lax.rem(r, 2)
    yp = lax.rem(r + 2, 4)
    dp = 3 - r
    has_left, has_right = p > 0, p < L - 1
    pos = (p, L - 1 - p)
    nxt = (f + 2, f - 2)

    def remote(src, dst, send, recv, **dev):
        return pltpu.make_async_remote_copy(
            src_ref=src, dst_ref=dst, send_sem=send, recv_sem=recv, device_id=dev, device_id_type=MESH
        )

    def signal(sem, **dev):
        pl.semaphore_signal(sem, inc=1, device_id=dev, device_id_type=MESH)

    def lanes(index):
        return pl.ds(pl.multiple_of(index * LANE, LANE), LANE)

    def block_rows(i):
        return pl.ds(pl.multiple_of(i * RB, RB), RB)

    def sub_rows(b):
        return pl.ds(b * SB, SB)

    def here_rows(u, b):
        return pl.ds(pl.multiple_of(lax.rem(u, NB) * RB + b * SB, SB), SB)

    def pool_load(tick, t):
        slot = lax.rem(tick, 2)
        rows_of = block_rows(lax.rem(lax.div(tick, L), NB))
        return pltpu.make_async_copy(pools[t].at[rows_of, :], pool_v.at[slot], pool_s.at[slot])

    def wf_loads(tick, t):
        j = lax.div(tick, L * NB)
        slot = lax.rem(tick, 2)
        core = jnp.where(lax.rem(tick, L) < 2, 1 - c, c)
        return [
            pltpu.make_async_copy(
                weights[t].at[:, lanes((2 * q + core) * NCH + j)],
                wf.at[slot, :, q * LANE : (q + 1) * LANE],
                wf_s.at[slot, q],
            )
            for q in range(L)
        ]

    def tower_of(index, start):
        for t in range(2):

            @pl.when(lax.rem(index, 2) == t)
            def _():
                start(t)

    def wb_loads(j, t):
        out = []
        for q in range(L):
            for k in range(2):
                out.append(
                    pltpu.make_async_copy(
                        weights[t].at[:, lanes((2 * q + k) * NCH + j)],
                        wb.at[q, :, k * LANE : (k + 1) * LANE],
                        wb_s.at[q, k],
                    )
                )
        return out

    def start_all(copies):
        for copy in copies:
            copy.start()

    def wait_all(copies):
        for copy in copies:
            copy.wait()

    def og_load(u, t):
        slot = lax.rem(u, 2)
        return pltpu.make_async_copy(
            ogs[t].at[block_rows(lax.rem(u, NB)), lanes(lax.div(u, NB))], og_v.at[slot, t], og_s.at[slot, t]
        )

    def mix_store(u, b, t):
        return pltpu.make_async_copy(
            mix_v.at[b, t], mixeds[t].at[here_rows(u, b), lanes(lax.div(u, NB))], mix_s.at[b, t]
        )

    def part_copy(u, t, par2):
        return remote(part_sib.at[t], xr.at[lax.rem(u, 3), t], xs_send.at[t], xs_recv.at[t, par2], feat=sib)

    def share_copy(u, o, core, d, b, s, par2):
        block = gath.at[lax.rem(lax.div(u, NB), 2), o, core, here_rows(u, b), :]
        return remote(block, block, g_send.at[d, b, s], g_recv.at[d, b, s, par2], feat=sib)

    def gath_copy(u, o, d, b, s, par2):
        block = gath.at[lax.rem(lax.div(u, NB), 2), o, c, here_rows(u, b), :]
        return remote(block, block, z_send.at[d, b, s], z_recv.at[d, b, s, par2], feat=nxt[d])

    def sum_copy(u, d, b, s, par2):
        u2 = lax.rem(u, 2)
        return remote(
            rbuf.at[u2, d, s - 1, sub_rows(b), :],
            rbuf.at[u2, d, s, sub_rows(b), :],
            z_send.at[d, b, s],
            z_recv.at[d, b, s, par2],
            feat=nxt[d],
        )

    def sum_wait(u, d, b, s, par2):
        block = rbuf.at[lax.rem(u, 2), d, s, sub_rows(b), :]
        remote(block, block, z_send.at[d, b, s], z_recv.at[d, b, s, par2], feat=nxt[d]).wait_recv()

    def own_sum(u, t, o, b):
        mine = part_own[lax.rem(u, 2), t, o, sub_rows(b), :].astype(F32)
        return mine + xr[lax.rem(u, 3), t, o, sub_rows(b), :].astype(F32)

    def fold(v):
        return jnp.sum(v.reshape(SB // 8, 8, LANE), axis=0)

    def finalize(u, b, per):
        j = lax.div(u, NB)
        last2 = lax.rem(per - 1, 2)

        @pl.when(has_left)
        def _():
            sum_wait(u, RIGHT, b, L - 1, last2)

        @pl.when(has_right)
        def _():
            sum_wait(u, LEFT, b, L - 1, last2)

        if b == 0:
            wait_all([og_load(u, 0), og_load(u, 1)])

        @pl.when(u >= 1)
        def _():
            wait_all([mix_store(u, b, 0), mix_store(u, b, 1)])

        u2 = lax.rem(u, 2)
        ch = lanes(j)
        s00, s01, s10, s11 = (par[k : k + 1, ch] for k in range(4))
        here = here_rows(u, b)
        row = scale[here, :]
        gy_a = row * og_v[u2, 0, sub_rows(b), :].astype(F32)
        gy_b = row * og_v[u2, 1, sub_rows(b), :].astype(F32)

        def gelu(t):
            v = own_sum(u, t, p, b) + par[4 + t : 5 + t, ch]
            for d in (RIGHT, LEFT):
                v = v + rbuf[u2, d, L - 1, sub_rows(b), t * LANE : (t + 1) * LANE].astype(F32)
            cdf = 0.5 * (1.0 + lax.erf(v * INV_SQRT2))
            return v * cdf, cdf + v * (INV_SQRT_2PI * jnp.exp(-0.5 * v * v))

        act_a, slope_a = gelu(0)
        act_b, slope_b = gelu(1)
        mix_v[b, 0] = (row * (s00 * act_a + s01 * act_b)).astype(BF16)
        mix_v[b, 1] = (row * (s10 * act_a + s11 * act_b)).astype(BF16)
        start_all([mix_store(u, b, 0), mix_store(u, b, 1)])
        gpre_a = ((s00 * gy_a + s10 * gy_b) * slope_a).astype(BF16)
        gpre_b = ((s01 * gy_a + s11 * gy_b) * slope_b).astype(BF16)
        gath[lax.rem(j, 2), p, c, here, :LANE] = gpre_a
        gath[lax.rem(j, 2), p, c, here, LANE:] = gpre_b
        sacc[j, 0] += fold(gy_a * act_a)
        sacc[j, 1] += fold(gy_a * act_b)
        sacc[j, 2] += fold(gy_b * act_a)
        sacc[j, 3] += fold(gy_b * act_b)
        sacc[j, 4] += fold(gpre_a.astype(F32))
        sacc[j, 5] += fold(gpre_b.astype(F32))

    first_partner, second_partner = (xp, yp), (yp, xp)

    def w_copy(t, kind):
        return remote(
            wsend.at[t, kind],
            wrecv.at[t, kind],
            w_send.at[t, kind],
            w_recv.at[t, kind],
            rows=second_partner[t] if kind == KEEP else first_partner[t],
        )

    def wout_stores(j, t):
        return [
            pltpu.make_async_copy(
                wout.at[t, :, k * LANE : (k + 1) * LANE], wgs[t].at[:, lanes(k * NCH + j)], wout_s.at[t, k]
            )
            for k in range(2)
        ]

    def pg_store(t, i, slot):
        dst = pl.ds(pl.multiple_of(i * PB, PB), PB)
        return pltpu.make_async_copy(pg_v.at[slot], pgs[t].at[dst, :], pg_s.at[slot])

    pool_load(0, 0).start()
    start_all(wf_loads(0, 0))

    bar = pltpu.get_barrier_semaphore()

    @pl.when(has_left)
    def _():
        signal(bar, feat=f - 2)

    @pl.when(has_right)
    def _():
        signal(bar, feat=f + 2)

    signal(bar, feat=sib)
    signal(bar, rows=xp)
    signal(bar, rows=yp)
    signal(bar, rows=dp)
    sacc[...] = jnp.zeros_like(sacc)

    @pl.when(jnp.logical_not(has_left))
    def _():
        for k in range(2):
            rbuf[k, RIGHT, L - 1] = jnp.zeros((RB, 2 * LANE), BF16)

    @pl.when(jnp.logical_not(has_right))
    def _():
        for k in range(2):
            rbuf[k, LEFT, L - 1] = jnp.zeros((RB, 2 * LANE), BF16)

    pl.semaphore_wait(bar, 4 + has_left.astype(jnp.int32) + has_right.astype(jnp.int32))

    def tick(T, carry):
        per, s = lax.div(T, L), lax.rem(T, L)
        par2 = lax.rem(per, 2)
        u = per - 2
        ur = per - 1
        uf = per
        gathers = (u >= 0) & (u < U)
        sums = (ur >= 0) & (ur < U)

        @pl.when((s == 0) & (per >= 1) & (per < SENDING))
        def _():
            @pl.when(has_left)
            def _():
                pl.semaphore_wait(credit.at[0], 1)

            @pl.when(has_right)
            def _():
                pl.semaphore_wait(credit.at[1], 1)

            pl.semaphore_wait(credit.at[2], 1)

        @pl.when((s == 1) & sums)
        def _():
            for t in range(2):
                part_copy(ur, t, lax.rem(per - 1, 2)).wait_recv()
            start_all([og_load(ur, 0), og_load(ur, 1)])

        for b in range(NS):

            @pl.when((s == 0) & gathers)
            def _():
                finalize(u, b, per)

            for d in (RIGHT, LEFT):
                gather_here = pos[d] >= s
                o = p - s if d == RIGHT else p + s
                dest = p + (L - s) if d == RIGHT else p - (L - s)
                shares = (s >= 1) if d == LEFT else (s >= 0)

                @pl.when(gathers & gather_here)
                def _():
                    @pl.when(s >= 1)
                    def _():
                        gath_copy(u, o, d, b, s - 1, par2).wait_recv()

                    @pl.when(pos[d] < L - 1)
                    def _():
                        gath_copy(u, o, d, b, s, par2).start()

                    @pl.when(shares)
                    def _():
                        share_copy(u, o, c, d, b, s, par2).start()

                @pl.when(sums & jnp.logical_not(gather_here))
                def _():
                    u2 = lax.rem(ur, 2)

                    @pl.when(pos[d] >= 1)
                    def _():
                        sum_wait(ur, d, b, s - 1, par2)
                        for t in range(2):
                            half = slice(t * LANE, (t + 1) * LANE)
                            both = own_sum(ur, t, dest, b) + rbuf[u2, d, s - 1, sub_rows(b), half].astype(F32)
                            rbuf[u2, d, s - 1, sub_rows(b), half] = both.astype(BF16)

                    @pl.when(pos[d] < 1)
                    def _():
                        for t in range(2):
                            half = slice(t * LANE, (t + 1) * LANE)
                            rbuf[u2, d, s - 1, sub_rows(b), half] = own_sum(ur, t, dest, b).astype(BF16)

                    sum_copy(ur, d, b, s, par2).start()

        @pl.when(uf < U)
        def _():
            pool_load(T, 0).wait()
            wait_all(wf_loads(T, 0))

            @pl.when(T + 1 < U * L)
            def _():
                def load(t):
                    pool_load(T + 1, t).start()
                    start_all(wf_loads(T + 1, t))

                tower_of(T + 1, load)

            t = lax.rem(s, 2)
            res = dot(pool_v[lax.rem(T, 2)], wf[lax.rem(T, 2)]).astype(BF16)

            @pl.when(s < 2)
            def _():
                for q in range(L):
                    part_sib[t, q] = res[:, q * LANE : (q + 1) * LANE]
                part_copy(uf, t, par2).start()

            @pl.when(s >= 2)
            def _():
                for q in range(L):
                    part_own[lax.rem(uf, 2), t, q] = res[:, q * LANE : (q + 1) * LANE]

            @pl.when((uf < NB) & (s >= 2))
            def _():
                pool_t[t, :, block_rows(uf)] = pool_v[lax.rem(T, 2)].T

        since = jnp.maximum(T - 2 * L, 0)
        jb = lax.div(since, NB * L) - 1
        tau = lax.rem(since, NB * L)
        jb2 = lax.rem(jb, 2)

        before = T - 1 + L
        per_m, s_m = lax.div(before, L) - 1, lax.rem(before, L)
        par_m = lax.rem(per_m + 2, 2)
        u_m, ur_m = per_m - 2, per_m - 1
        gathers_m = (u_m >= 0) & (u_m < U)
        sums_m = (ur_m >= 0) & (ur_m < U)
        for b in range(NS):
            for d in (RIGHT, LEFT):
                o = p - s_m if d == RIGHT else p + s_m
                shares = (s_m >= 1) if d == LEFT else (s_m >= 0)

                @pl.when(gathers_m & (pos[d] >= s_m) & shares)
                def _():
                    share_copy(u_m, o, 1 - c, d, b, s_m, par_m).wait_recv()

        @pl.when(jb >= 0)
        def _():
            @pl.when((tau == 0) & (jb >= 1))
            def _():
                for k in range(2):
                    pl.semaphore_wait(wcredit.at[0, k], 1)

            @pl.when((tau == 1) & (jb >= 1))
            def _():
                for k in range(2):
                    pl.semaphore_wait(wcredit.at[1, k], 1)

            @pl.when(tau == 3)
            def _():
                start_all(wb_loads(jb, 0))

            @pl.when(tau < 4)
            def _():
                for t in range(2):
                    one, two = first_partner[t], second_partner[t]
                    owner = jnp.where(
                        tau == FAR, dp, jnp.where(tau == NEAR, one, jnp.where(tau == KEEP, two, r))
                    )
                    cols = [gath[jb2, owner, k, :, t * LANE : (t + 1) * LANE] for k in range(2)]
                    cols = jnp.concatenate(cols, axis=1)
                    wsend[t, tau] = dot(pool_t[t], cols).astype(BF16)
                    for way in (FAR, NEAR):

                        @pl.when(tau == way)
                        def _():
                            w_copy(t, way).start()

            @pl.when(tau == 4)
            def _():
                for t in range(2):
                    w_copy(t, FAR).wait_recv()
                    both = wsend[t, KEEP].astype(F32) + wrecv[t, FAR].astype(F32)
                    wsend[t, KEEP] = both.astype(BF16)
                    w_copy(t, KEEP).start()

                @pl.when(jb < NCH - 1)
                def _():
                    signal(wcredit.at[0, 0], rows=xp)
                    signal(wcredit.at[0, 1], rows=yp)

            @pl.when(tau >= 4)
            def _():
                t = lax.rem(tau, 2)
                wait_all(wb_loads(jb, 0))
                for k in range(2):
                    i = 2 * lax.div(tau - 4, 2) + k
                    mine = pl.ds(pl.multiple_of(i * PB, PB), PB)
                    total = None
                    for q in range(L):
                        cols = [gath[jb2, q, core, mine, lanes(t)] for core in range(2)]
                        term = dot_t(jnp.concatenate(cols, axis=1), wb[q])
                        total = term if total is None else total + term

                    @pl.when(jb == 0)
                    def _():
                        acc[t, mine, :] = total

                    @pl.when((jb > 0) & (jb < NCH - 1))
                    def _():
                        acc[t, mine, :] += total

                    @pl.when(jb == NCH - 1)
                    def _():
                        @pl.when(tau >= 5)
                        def _():
                            pg_store(0, 0, k).wait()

                        pg_v[k] = (acc[t, mine, :] + total).astype(BF16)

                        def store(tt):
                            pg_store(tt, i, k).start()

                        tower_of(tau, store)

                @pl.when(tau < 7)
                def _():
                    tower_of(tau + 1, lambda tt: start_all(wb_loads(jb, tt)))

            @pl.when(tau == 7)
            def _():
                for t in range(2):
                    w_copy(t, NEAR).wait_recv()
                    w_copy(t, KEEP).wait_recv()
                    for kind in (FAR, NEAR, KEEP):
                        w_copy(t, kind).wait_send()

                    @pl.when(jb >= 1)
                    def _():
                        wait_all(wout_stores(jb, t))

                    both = wsend[t, OWN].astype(F32) + wrecv[t, NEAR].astype(F32)
                    wout[t] = both + wrecv[t, KEEP].astype(F32)
                    start_all(wout_stores(jb, t))

                @pl.when(jb < NCH - 1)
                def _():
                    signal(wcredit.at[1, 0], rows=xp)
                    signal(wcredit.at[1, 1], rows=yp)

        @pl.when((per_m >= 0) & (per_m < U) & (s_m < 2))
        def _():
            part_copy(per_m, lax.rem(s_m, 2), par_m).wait_send()

        for b in range(NS):
            for d in (RIGHT, LEFT):
                shares = (s_m >= 1) if d == LEFT else (s_m >= 0)

                @pl.when(gathers_m & (pos[d] >= s_m))
                def _():
                    @pl.when(pos[d] < L - 1)
                    def _():
                        gath_copy(u_m, p, d, b, s_m, par_m).wait_send()

                    @pl.when(shares)
                    def _():
                        share_copy(u_m, p, c, d, b, s_m, par_m).wait_send()

                @pl.when(sums_m & (pos[d] < s_m))
                def _():
                    sum_copy(ur_m, d, b, s_m, par_m).wait_send()

        @pl.when((s == 1) & (per < SENDING - 1))
        def _():
            @pl.when(has_left)
            def _():
                signal(credit.at[1], feat=f - 2)

            @pl.when(has_right)
            def _():
                signal(credit.at[0], feat=f + 2)

            signal(credit.at[2], feat=sib)

        @pl.when(T == (U + 1) * L + 1)
        def _():
            for j in range(NCH):
                for k in range(6):
                    sred[j, k : k + 1, :] = jnp.sum(sacc[j, k], axis=0, keepdims=True)
                sred[j, 6:8, :] = jnp.zeros((2, LANE), F32)
            for k, peer in enumerate((xp, yp, dp)):
                remote(sred.at[peer], srecv.at[k], st_send.at[k], st_recv.at[k], rows=peer).start()

        return carry

    lax.fori_loop(0, TICKS, tick, 0)

    for k, peer in enumerate((xp, yp, dp)):
        copy = remote(sred.at[peer], srecv.at[k], st_send.at[k], st_recv.at[k], rows=peer)
        copy.wait_send()
        copy.wait_recv()
    stats[...] = sred[r] + srecv[0] + srecv[1] + srecv[2]
    for t in range(2):
        for b in range(NS):
            mix_store(U - 1, b, t).wait()
        wait_all(wout_stores(NCH - 1, t))
        pg_store(0, 0, t).wait()


def fused(pool_a, pool_b, weight_a, weight_b, bias_a, bias_b, stitch, row_scale, outgrad_a, outgrad_b):
    rows, width = pool_a.shape
    chl = bias_a.shape[0]
    NB, NS, L = ROW_BLOCKS, SUBS, 4
    RB = rows // NB
    SB = RB // NS
    NCH = chl // LANE
    par = jnp.concatenate([stitch.reshape(4, chl), bias_a[None], bias_b[None], jnp.zeros((2, chl), F32)], axis=0)
    hbm = pl.BlockSpec(memory_space=pl.ANY)
    vmem = pl.BlockSpec(memory_space=pltpu.VMEM)
    dma = pltpu.SemaphoreType.DMA
    out_shape = (
        jax.ShapeDtypeStruct((rows, chl), BF16),
        jax.ShapeDtypeStruct((rows, chl), BF16),
        jax.ShapeDtypeStruct((rows, width), BF16),
        jax.ShapeDtypeStruct((rows, width), BF16),
        jax.ShapeDtypeStruct((width, 2 * chl), F32),
        jax.ShapeDtypeStruct((width, 2 * chl), F32),
        jax.ShapeDtypeStruct((8, LANE), F32),
    )
    scratch = [
        pltpu.VMEM((2, RB, width), BF16),
        pltpu.VMEM((2, width, rows), BF16),
        pltpu.VMEM((2, width, L * LANE), BF16),
        pltpu.VMEM((L, width, 2 * LANE), BF16),
        pltpu.VMEM((2, L, RB, LANE), BF16),
        pltpu.VMEM((2, 2, L, RB, LANE), BF16),
        pltpu.VMEM((3, 2, L, RB, LANE), BF16),
        pltpu.VMEM((2, 2, L, RB, 2 * LANE), BF16),
        pltpu.VMEM((2, L, 2, rows, 2 * LANE), BF16),
        pltpu.VMEM((2, rows, width), F32),
        pltpu.VMEM((2, 4, width, 2 * LANE), BF16),
        pltpu.VMEM((2, 3, width, 2 * LANE), BF16),
        pltpu.VMEM((2, width, 2 * LANE), F32),
        pltpu.VMEM((2, 2, RB, LANE), BF16),
        pltpu.VMEM((NS, 2, SB, LANE), BF16),
        pltpu.VMEM((2, rows // PIECES, width), BF16),
        pltpu.VMEM((NCH, 6, 8, LANE), F32),
        pltpu.VMEM((NCH, 8, LANE), F32),
        pltpu.VMEM((3, 8, LANE), F32),
        dma((2,)),
        dma((2, L)),
        dma((L, 2)),
        dma((2,)),
        dma((2, 2)),
        dma((2, NS, L)),
        dma((2, NS, L, 2)),
        dma((2, NS, L)),
        dma((2, NS, L, 2)),
        dma((2, 3)),
        dma((2, 3)),
        dma((2, 2)),
        dma((2, 2)),
        dma((NS, 2)),
        dma((2,)),
        dma((3,)),
        dma((3,)),
        pltpu.SemaphoreType.REGULAR((3,)),
        pltpu.SemaphoreType.REGULAR((2, 2)),
    ]
    mixed_a, mixed_b, pg_a, pg_b, wg_a, wg_b, stats = pl.pallas_call(
        functools.partial(kernel, rows, width, chl),
        out_shape=out_shape,
        in_specs=[hbm, hbm, hbm, hbm, vmem, vmem, hbm, hbm],
        out_specs=(hbm, hbm, hbm, hbm, hbm, hbm, vmem),
        scratch_shapes=scratch,
        compiler_params=pltpu.CompilerParams(
            collective_id=0, has_side_effects=True, vmem_limit_bytes=VMEM_LIMIT
        ),
    )(pool_a, pool_b, weight_a, weight_b, par, row_scale[:, None], outgrad_a, outgrad_b)
    return mixed_a, mixed_b, pg_a, pg_b, wg_a, wg_b, stats[4], stats[5], stats[:4].reshape(2, 2, LANE)


VMEM_LIMIT = 63 * 1024 * 1024


def plain(pool_a, pool_b, weight_a, weight_b, bias_a, bias_b, stitch, row_scale, outgrad_a, outgrad_b):
    row = row_scale[:, None]

    def pre(pool, weight, bias):
        partial = dot(pool, weight).astype(BF16)
        return lax.psum_scatter(partial, "feat", scatter_dimension=1, tiled=True).astype(F32) + bias

    def gelu(v):
        cdf = 0.5 * (1.0 + lax.erf(v * INV_SQRT2))
        return v * cdf, cdf + v * (INV_SQRT_2PI * jnp.exp(-0.5 * v * v))

    act_a, slope_a = gelu(pre(pool_a, weight_a, bias_a))
    act_b, slope_b = gelu(pre(pool_b, weight_b, bias_b))
    (s00, s01), (s10, s11) = stitch[0], stitch[1]
    mixed_a = (row * (s00 * act_a + s01 * act_b)).astype(BF16)
    mixed_b = (row * (s10 * act_a + s11 * act_b)).astype(BF16)
    gy_a = row * outgrad_a.astype(F32)
    gy_b = row * outgrad_b.astype(F32)
    gpre_a = ((s00 * gy_a + s10 * gy_b) * slope_a).astype(BF16)
    gpre_b = ((s01 * gy_a + s11 * gy_b) * slope_b).astype(BF16)
    sums = jnp.stack(
        [
            jnp.sum(v, axis=0)
            for v in (
                gy_a * act_a,
                gy_a * act_b,
                gy_b * act_a,
                gy_b * act_b,
                gpre_a.astype(F32),
                gpre_b.astype(F32),
            )
        ]
    )
    sums = lax.psum_scatter(sums, "rows", scatter_dimension=1, tiled=True)

    def back(pool, weight, gpre):
        whole = lax.all_gather(gpre, "feat", axis=1, tiled=True)
        pool_grad = dot_t(whole, weight).astype(BF16)
        wgrad = lax.dot_general(pool, whole, (((0,), (0,)), ((), ())), preferred_element_type=F32)
        wgrad = lax.psum_scatter(wgrad.astype(BF16), "rows", scatter_dimension=1, tiled=True)
        return pool_grad, wgrad.astype(F32)

    pg_a, wg_a = back(pool_a, weight_a, gpre_a)
    pg_b, wg_b = back(pool_b, weight_b, gpre_b)
    return mixed_a, mixed_b, pg_a, pg_b, wg_a, wg_b, sums[4], sums[5], sums[:4].reshape(2, 2, -1)


def shards(
    pool_a, pool_b, weight_a, weight_b, bias_a, bias_b, stitch, crop_count, row_mask, outgrad_a, outgrad_b
):
    row_scale = row_mask.astype(F32) / crop_count.astype(F32)
    rows, width = pool_a.shape
    chl = bias_a.shape[0]
    n_rows, n_feat = lax.axis_size("rows"), lax.axis_size("feat")
    fits = (
        n_rows == 4
        and n_feat == 8
        and chl == n_rows * LANE
        and width % LANE == 0
        and rows % (ROW_BLOCKS * SUBS * LANE) == 0
    )
    run = fused if fits else plain
    return run(pool_a, pool_b, weight_a, weight_b, bias_a, bias_b, stitch, row_scale, outgrad_a, outgrad_b)


def solution(mesh):
    return jax.shard_map(
        shards,
        mesh=mesh,
        in_specs=(
            P("rows", "feat"),
            P("rows", "feat"),
            P("feat", None),
            P("feat", None),
            P("feat"),
            P("feat"),
            P(None, None, "feat"),
            P("rows"),
            P("rows"),
            P("rows", "feat"),
            P("rows", "feat"),
        ),
        out_specs=(
            P("rows", "feat"),
            P("rows", "feat"),
            P("rows", "feat"),
            P("rows", "feat"),
            P("feat", "rows"),
            P("feat", "rows"),
            P(("feat", "rows")),
            P(("feat", "rows")),
            P(None, None, ("feat", "rows")),
        ),
        check_vma=False,
    )
```

time: 394 us -> 328 us (0.83)
  Pallas kernels: 371 us -> 305 us
    pallas_call x1, Pallas kernels: 371 us -> 305 us  [fused(): pl.pallas_call(functools.partial(kernel, rows, width, chl), out_shape=out...]
where the time goes in v2:
time: 328 us; the launch traced here: 327 us
  Pallas kernels  305 us (93%)
  local copies, waits for them, and re-layouts  19.8 us (6%)
    pallas_call x1, Pallas kernels, fused(): pl.pallas_call(functools.partial(kernel, rows, width, chl), out_shape=out...  305 us
    unnamed x18, local copies, waits for them, and re-layouts  15.3 us

profile of v2, /device:TPU:0, one launch (start us, length us, event | category | flops | bytes accessed | tf_op | source)
XLA Modules:
  0.0 327.2 jit_solution(2564058249480647940)
XLA Ops:
  0.7 0.1 pad.3.clone
  0.7 0.7 reshape.24
  1.4 1.4 maximum_maximum_fusion.refs_4_
  2.8 0.7 convert_divide_fusion
  3.5 1.1 broadcast_in_dim.16.refs_5_
  4.6 304.6 %shard_map.178 = (bf16[1280,512]{1,0:T(8,128)(2,1)}, bf16[1280,512]{1,0:T(8,128)(2,1)}, bf16[1280,1152]{1,0:T(8,128)(2,1)}, bf16[1280,1152]{1,0:T(8,128)(2,1)}, ...) custom-call(bf16[1280,1152]{1,0:T(8,128)(2,1)} %refs_0_.1, bf16[1280,1152]{1,0:T(8,128)(2,1)} %refs_1_.1, ...), custom_call_target="tpu_custom_call" | custom-call | tf_op jit(solution)/shard_map/pallas_call | solution.py:626
  309.2 0.0 copy-start.1
  309.2 1.4 slice_bitcast_fusion
  310.6 1.3 slice.11
  311.8 2.5 copy.27
  314.3 0.0 slice-start.2
  314.3 2.6 copy.28
  316.9 0.0 copy-done.1
  316.9 0.0 copy-start
  316.9 0.0 slice-start.3
  316.9 1.6 copy.29
  318.5 1.3 copy-done
  319.8 0.0 slice-start
  319.8 1.6 copy.30
  321.4 0.0 slice-done.2
  321.4 0.0 slice-done.3
  321.4 0.0 slice-start.1
  321.4 2.4 copy.31
  323.8 1.0 slice-done
  324.8 0.2 slice-done.1
  325.0 2.2 copy.32
  (3 shorter events, 0.0 us)
Async XLA Ops:
  309.2 7.7 %copy-start.1 = (bf16[1280,1152]{1,0:T(8,128)(2,1)S(1)}, bf16[1280,1152]{1,0:T(8,128)(2,1)}, u32[]{:S(2)}) copy-start(bf16[1280,1152]{1,0:T(8,128)(2,1)} %get-tuple-element.36) | copy-start | bytes 8847364
  314.3 7.1 %slice-start.2 = ((s8[4718592]{0:T(1024)(128)(4,1)}), s8[4194304]{0:T(1024)(128)(4,1)S(1)}, s32[]{:S(2)}) async-start(s8[4718592]{0:T(1024)(128)(4,1)} %bitcast.9), calls=%async_computation.2 | async-start | bytes 8388608
  316.9 2.9 copy-start
  316.9 4.5 %slice-start.3 = ((s8[4718592]{0:T(1024)(128)(4,1)}), s8[524288]{0:T(1024)(128)(4,1)S(1)}, s32[]{:S(2)}) async-start(s8[4718592]{0:T(1024)(128)(4,1)} %bitcast.9), calls=%async_computation.3 | async-start | bytes 1048576
  319.8 5.0 %slice-start = ((s8[4718592]{0:T(1024)(128)(4,1)}), s8[4194304]{0:T(1024)(128)(4,1)S(1)}, s32[]{:S(2)}) async-start(s8[4718592]{0:T(1024)(128)(4,1)} %bitcast.7), calls=%async_computation | async-start | bytes 8388608
  321.4 3.6 %slice-start.1 = ((s8[4718592]{0:T(1024)(128)(4,1)}), s8[524288]{0:T(1024)(128)(4,1)S(1)}, s32[]{:S(2)}) async-start(s8[4718592]{0:T(1024)(128)(4,1)} %bitcast.7), calls=%async_computation.1 | async-start | bytes 1048576

commit v3 on v2

v3 whole, which is shorter than its diff:
```python
import functools

import jax
import jax.numpy as jnp
from jax import lax
from jax.experimental import pallas as pl
from jax.experimental.pallas import tpu as pltpu
from jax.sharding import PartitionSpec as P

MESH = pl.DeviceIdType.MESH
F32 = jnp.float32
BF16 = jnp.bfloat16
LANE = 128
HALF = 64
SUBS = 5
PIECES = 4
RIGHT, LEFT = 0, 1
FAR, NEAR, KEEP, OWN = 0, 1, 2, 3
INV_SQRT2 = 0.7071067811865476
INV_SQRT_2PI = 0.3989422804014327


def dot(lhs, rhs):
    return lax.dot_general(lhs, rhs, (((1,), (0,)), ((), ())), preferred_element_type=F32)


def dot_t(lhs, rhs):
    return lax.dot_general(lhs, rhs, (((1,), (1,)), ((), ())), preferred_element_type=F32)


def swap(v):
    return pltpu.roll(v, HALF, 1)


def upper(rows):
    return lax.broadcasted_iota(jnp.int32, (rows, LANE), 1) >= HALF


def halves(one, two, half):
    if half == 0:
        return jnp.where(upper(one.shape[0]), swap(two), one)
    return jnp.where(upper(one.shape[0]), two, swap(one))


def kernel(rows, width, chl, *refs):
    (
        pool_a, pool_b, weight_a, weight_b, bias_a, bias_b, stitch, mask, count, og_a, og_b,
        mixed_a, mixed_b, pg_a, pg_b, wg_a, wg_b, stats,
        pool_v, pool_t, wf, wb, part_sib, part_own, xr, rbuf, gath, acc, wsend, wkeep, wrecv, wout,
        og_v, scale, par, mix_0, mix_v, sacc, sred, srecv,
        pool_s, wf_s, wb_s, xs_send, xs_recv, z_send, z_recv, g_send, g_recv,
        w_send, w_recv, wout_s, og_s, mix_s, pg_s, st_send, st_recv, credit, wcredit,
    ) = refs
    L = 4
    NS = SUBS
    SB = rows // NS
    HB = rows // 2
    PB = rows // PIECES
    NCH = chl // LANE
    U = 2 * NCH
    SENDING = U + 3
    TICKS = (U + 5) * L
    pools, weights = (pool_a, pool_b), (weight_a, weight_b)
    ogs, mixeds = (og_a, og_b), (mixed_a, mixed_b)
    pgs, wgs = (pg_a, pg_b), (wg_a, wg_b)

    f = lax.axis_index("feat")
    r = lax.axis_index("rows")
    p = lax.div(f, 2)
    c = lax.rem(f, 2)
    sib = f + 1 - 2 * c
    xp = r + 1 - 2 * lax.rem(r, 2)
    yp = lax.rem(r + 2, 4)
    dp = 3 - r
    has_left, has_right = p > 0, p < L - 1
    pos = (p, L - 1 - p)
    has_up = (has_left, has_right)
    nxt = (f + 2, f - 2)

    def remote(src, dst, send, recv, **dev):
        return pltpu.make_async_remote_copy(
            src_ref=src, dst_ref=dst, send_sem=send, recv_sem=recv, device_id=dev, device_id_type=MESH
        )

    def signal(sem, **dev):
        pl.semaphore_signal(sem, inc=1, device_id=dev, device_id_type=MESH)

    def start_all(copies):
        for copy in copies:
            copy.start()

    def wait_all(copies):
        for copy in copies:
            copy.wait()

    def lanes(index):
        return pl.ds(pl.multiple_of(index * LANE, LANE), LANE)

    def some_rows(i, n):
        return pl.ds(pl.multiple_of(i * n, n), n)

    def sub_rows(b):
        return pl.ds(b * SB, SB)

    def tower_of(index, run):
        for t in range(2):

            @pl.when(lax.rem(index, 2) == t)
            def _():
                run(t)

    def pool_load(tick, t):
        slot = lax.rem(tick, 2)
        half = lax.div(lax.rem(tick, L), 2)
        return pltpu.make_async_copy(pools[t].at[some_rows(half, HB), :], pool_v.at[slot], pool_s.at[slot])

    def wf_loads(tick, t):
        j = lax.div(tick, 2 * L)
        slot = lax.rem(tick, 2)
        core = jnp.where(lax.rem(lax.div(tick, L), 2) == 0, c, 1 - c)
        return [
            pltpu.make_async_copy(
                weights[t].at[:, lanes((2 * q + core) * NCH + j)],
                wf.at[slot, :, q * LANE : (q + 1) * LANE],
                wf_s.at[slot, q],
            )
            for q in range(L)
        ]

    def wb_loads(j, t):
        out = []
        for q in range(L):
            for k in range(2):
                out.append(
                    pltpu.make_async_copy(
                        weights[t].at[:, lanes((2 * q + k) * NCH + j)],
                        wb.at[q, :, k * LANE : (k + 1) * LANE],
                        wb_s.at[q, k],
                    )
                )
        return out

    def og_loads(j):
        return [pltpu.make_async_copy(ogs[t].at[:, lanes(j)], og_v.at[t], og_s.at[t]) for t in range(2)]

    def mix_stores(j, b):
        return [
            pltpu.make_async_copy(mix_v.at[b % 2, t], mixeds[t].at[sub_rows(b), lanes(j)], mix_s.at[b % 2, t])
            for t in range(2)
        ]

    def part_copy(j, s, slot):
        t, half = lax.rem(s, 2), lax.div(s, 2)
        return remote(
            part_sib.at[slot],
            xr.at[lax.rem(j, 2), t, :, some_rows(half, HB), :],
            xs_send.at[s],
            xs_recv.at[s],
            feat=sib,
        )

    def share_copy(u, o, core, d, b, s, par2):
        block = gath.at[lax.rem(u, 4), o, core, sub_rows(b), :]
        return remote(block, block, g_send.at[d, b, s], g_recv.at[d, b, s, par2], feat=sib)

    def gath_copy(u, o, d, b, s, par2):
        block = gath.at[lax.rem(u, 4), o, c, sub_rows(b), :]
        return remote(block, block, z_send.at[d, b, s], z_recv.at[d, b, s, par2], feat=nxt[d])

    def sum_block(u, d, b, s):
        return rbuf.at[lax.rem(u, 2), d, lax.rem(s, 3), sub_rows(b), :]

    def sum_copy(u, d, b, s, par2):
        return remote(
            sum_block(u, d, b, s - 1),
            sum_block(u, d, b, s),
            z_send.at[d, b, s],
            z_recv.at[d, b, s, par2],
            feat=nxt[d],
        )

    def sum_wait(u, d, b, s, par2):
        block = sum_block(u, d, b, s)
        remote(block, block, z_send.at[d, b, s], z_recv.at[d, b, s, par2], feat=nxt[d]).wait_recv()

    def packed(one, two, h):
        return jnp.where(upper(one.shape[0]) == (h == 1), one, swap(two))

    def own_sum(u, o, b):
        j, h = lax.div(u, 2), lax.rem(u, 2)
        j2 = lax.rem(j, 2)

        def tower(t):
            return part_own[j2, t, o, sub_rows(b), :].astype(F32) + xr[j2, t, o, sub_rows(b), :].astype(F32)

        return packed(tower(h), tower(1 - h), h)

    def fold(v):
        return jnp.sum(v.reshape(SB // 8, 8, LANE), axis=0)

    def finalize(u, b, per):
        j, h = lax.div(u, 2), lax.rem(u, 2)
        last2 = lax.rem(per - 1, 2)
        for d in (RIGHT, LEFT):

            @pl.when(has_up[d])
            def _():
                sum_wait(u, d, b, L - 1, last2)

        if b == 0:

            @pl.when(h == 0)
            def _():
                wait_all(og_loads(j))

        v = own_sum(u, p, b) + par[u, 3:4, :]
        for d in (RIGHT, LEFT):
            v = v + jnp.where(has_up[d], rbuf[lax.rem(u, 2), d, 0, sub_rows(b), :].astype(F32), 0.0)
        same, cross, back = (par[u, k : k + 1, :] for k in range(3))
        row = jnp.concatenate(
            [jnp.broadcast_to(scale[k : k + 1, :], (LANE, LANE)).T for k in range(b * SB // LANE, (b + 1) * SB // LANE)],
            axis=0,
        )
        gy = row * packed(og_v[h, sub_rows(b), :].astype(F32), og_v[1 - h, sub_rows(b), :].astype(F32), h)
        cdf = 0.5 * (1.0 + lax.erf(v * INV_SQRT2))
        act = v * cdf
        slope = cdf + v * (INV_SQRT_2PI * jnp.exp(-0.5 * v * v))
        act_x = swap(act)
        mixed = row * (same * act + cross * act_x)
        gpre = ((same * gy + back * swap(gy)) * slope).astype(BF16)
        gath[lax.rem(u, 4), p, c, sub_rows(b), :] = gpre
        sacc[u, 0] += fold(gy * act)
        sacc[u, 1] += fold(gy * act_x)
        sacc[u, 2] += fold(gpre.astype(F32))

        @pl.when(h == 0)
        def _():
            mix_0[sub_rows(b), :] = mixed.astype(BF16)

        @pl.when(h == 1)
        def _():
            if b > 1:
                wait_all(mix_stores(j, b))
            else:

                @pl.when(j >= 1)
                def _():
                    wait_all(mix_stores(j, b))

            first, second = mix_0[sub_rows(b), :], mixed.astype(BF16)
            for t in range(2):
                mix_v[b % 2, t] = halves(first, second, t)
            start_all(mix_stores(j, b))

    first_partner, second_partner = (xp, yp), (yp, xp)

    def w_copy(u, t, kind):
        u2 = lax.rem(u, 2)
        return remote(
            wkeep.at[u2, t, 0] if kind == KEEP else wsend.at[t, kind],
            wrecv.at[u2, t, kind],
            w_send.at[t, kind],
            w_recv.at[u2, t, kind],
            rows=second_partner[t] if kind == KEEP else first_partner[t],
        )

    def wout_stores(j, t):
        return [
            pltpu.make_async_copy(wout.at[t, k], wgs[t].at[:, lanes(k * NCH + j)], wout_s.at[t, k])
            for k in range(2)
        ]

    def pg_place(i):
        return pool_v.at[lax.div(i, 2), some_rows(lax.rem(i, 2), PB), :]

    def pg_store(t, i):
        return pltpu.make_async_copy(pg_place(i), pgs[t].at[some_rows(i, PB), :], pg_s.at[i])

    def row_products(u, t, one, two):
        cols = []
        for owner in (one, two):
            pair = [gath[lax.rem(u, 4), owner, core] for core in range(2)]
            cols.append(halves(pair[0], pair[1], t))
        return dot(pool_t[t], jnp.concatenate(cols, axis=1)).astype(BF16)

    def pool_products(j, t, i):
        mine = some_rows(i, PB)
        total = None
        for q in range(L):
            cols = []
            for core in range(2):
                pair = [gath[lax.rem(2 * j + h, 4), q, core, mine, :] for h in range(2)]
                cols.append(halves(pair[0], pair[1], t))
            term = dot_t(jnp.concatenate(cols, axis=1), wb[q])
            total = term if total is None else total + term

        @pl.when(j == 0)
        def _():
            acc[t, mine, :] = total

        @pl.when((j > 0) & (j < NCH - 1))
        def _():
            acc[t, mine, :] += total

        @pl.when(j == NCH - 1)
        def _():
            if t > 0:
                pg_store(t, i).wait()
            pg_place(i)[...] = (acc[t, mine, :] + total).astype(BF16)
            pg_store(t, i).start()

    pool_load(0, 0).start()
    start_all(wf_loads(0, 0))

    bar = pltpu.get_barrier_semaphore()

    @pl.when(has_left)
    def _():
        signal(bar, feat=f - 2)

    @pl.when(has_right)
    def _():
        signal(bar, feat=f + 2)

    signal(bar, feat=sib)
    signal(bar, rows=xp)
    signal(bar, rows=yp)
    signal(bar, rows=dp)
    sacc[...] = jnp.zeros_like(sacc)
    for k in range(rows // LANE):
        here = slice(k * LANE, (k + 1) * LANE)
        scale[k : k + 1, :] = mask[:, here].astype(F32) / count[:, here].astype(F32)
    for u in range(U):
        ch = slice(u // 2 * LANE, (u // 2 + 1) * LANE)
        s00, s01, s10, s11 = (stitch[k : k + 1, ch] for k in range(4))
        rows_of = (s00, s11), (s01, s10), (s10, s01), (bias_a[:, ch], bias_b[:, ch])
        for k, (one, two) in enumerate(rows_of):
            par[u, k : k + 1, :] = halves(one, two, u % 2)

    pl.semaphore_wait(bar, 4 + has_left.astype(jnp.int32) + has_right.astype(jnp.int32))

    def tick(T, carry):
        per, s = lax.div(T, L), lax.rem(T, L)
        par2 = lax.rem(per, 2)
        u = per - 3
        ur = per - 2
        gathers = (u >= 0) & (u < U)
        sums = (ur >= 0) & (ur < U)

        @pl.when((s == 0) & (per >= 1) & (per < SENDING))
        def _():
            @pl.when(has_left)
            def _():
                pl.semaphore_wait(credit.at[0], 1)

            @pl.when(has_right)
            def _():
                pl.semaphore_wait(credit.at[1], 1)

            pl.semaphore_wait(credit.at[2], 1)

        @pl.when((s == 1) & sums & (par2 == 0))
        def _():
            for k in range(L):
                part_copy(lax.div(ur, 2), k, 0).wait_recv()
            start_all(og_loads(lax.div(ur, 2)))

        before = T - 1 + L
        per_m, s_m = lax.div(before, L) - 1, lax.rem(before, L)
        par_m = lax.rem(per_m + 2, 2)
        u_m, ur_m = per_m - 3, per_m - 2
        gathers_m = (u_m >= 0) & (u_m < U)
        sums_m = (ur_m >= 0) & (ur_m < U)
        ub = per - 4
        uz = per - 5
        jp = lax.div(jnp.maximum(per - 5, 0), 2)

        def flows(b):
            @pl.when((s == 0) & gathers)
            def _():
                finalize(u, b, per)

            for d in (RIGHT, LEFT):
                gather_here = pos[d] >= s
                o = p - s if d == RIGHT else p + s
                dest = p + (L - s) if d == RIGHT else p - (L - s)
                shares = (s >= 1) if d == LEFT else (s >= 0)

                @pl.when(gathers & gather_here)
                def _():
                    @pl.when(s >= 1)
                    def _():
                        gath_copy(u, o, d, b, s - 1, par2).wait_recv()

                    @pl.when(pos[d] < L - 1)
                    def _():
                        gath_copy(u, o, d, b, s, par2).start()

                    @pl.when(shares)
                    def _():
                        share_copy(u, o, c, d, b, s, par2).start()

                @pl.when(sums & jnp.logical_not(gather_here))
                def _():
                    block = sum_block(ur, d, b, s - 1)

                    @pl.when(pos[d] >= 1)
                    def _():
                        sum_wait(ur, d, b, s - 1, par2)
                        block[...] = (own_sum(ur, dest, b) + block[...].astype(F32)).astype(BF16)

                    @pl.when(pos[d] < 1)
                    def _():
                        block[...] = own_sum(ur, dest, b).astype(BF16)

                    sum_copy(ur, d, b, s, par2).start()

        def share_waits():
            for b in range(NS):
                for d in (RIGHT, LEFT):
                    o = p - s_m if d == RIGHT else p + s_m
                    shares = (s_m >= 1) if d == LEFT else (s_m >= 0)

                    @pl.when(gathers_m & (pos[d] >= s_m) & shares)
                    def _():
                        share_copy(u_m, o, 1 - c, d, b, s_m, par_m).wait_recv()

        def partial_products():
            @pl.when(per < U)
            def _():
                slot = lax.rem(T, 2)
                pool_load(T, 0).wait()
                wait_all(wf_loads(T, 0))

                @pl.when(T + 1 < U * L)
                def _():
                    def load(t):
                        pool_load(T + 1, t).start()
                        start_all(wf_loads(T + 1, t))

                    tower_of(T + 1, load)

                j = lax.div(per, 2)
                t, half = lax.rem(s, 2), lax.div(s, 2)
                res = dot(pool_v[slot], wf[slot]).astype(BF16)

                @pl.when(par2 == 0)
                def _():
                    for q in range(L):
                        part_own[lax.rem(j, 2), t, q, some_rows(half, HB), :] = res[:, q * LANE : (q + 1) * LANE]

                @pl.when(par2 == 1)
                def _():
                    for q in range(L):
                        part_sib[slot, q] = res[:, q * LANE : (q + 1) * LANE]
                    part_copy(j, s, slot).start()

                @pl.when(per == 0)
                def _():
                    pool_t[t, :, some_rows(half, HB)] = pool_v[slot].T

        def weight_products(t):
            @pl.when((s == 0) & (ub >= 0) & (ub < U))
            def _():
                if t == 0:

                    @pl.when(ub >= 2)
                    def _():
                        pl.semaphore_wait(wcredit.at[0], 1)
                        pl.semaphore_wait(wcredit.at[1], 1)

                res = row_products(ub, t, dp, first_partner[t])
                for kind in (FAR, NEAR):
                    wsend[t, kind] = res[:, kind * LANE : (kind + 1) * LANE]
                    w_copy(ub, t, kind).start()

            @pl.when((s == 1) & (ub >= 0) & (ub < U))
            def _():
                res = row_products(ub, t, second_partner[t], r)
                for k in range(2):
                    wkeep[lax.rem(ub, 2), t, k] = res[:, k * LANE : (k + 1) * LANE]

        def pool_piece(k):
            @pl.when((per >= 5) & (par2 == 1) & (s >= 2))
            def _():
                if k == 0:

                    @pl.when(s == 2)
                    def _():
                        wait_all(wb_loads(jp, 0))

                pool_products(jp, 0, 2 * (s - 2) + k)
                if k == 1:

                    @pl.when(s == 3)
                    def _():
                        start_all(wb_loads(jp, 1))

            @pl.when((per >= 6) & (par2 == 0) & ((s == 1) | (s == 2)))
            def _():
                if k == 0:

                    @pl.when(s == 1)
                    def _():
                        wait_all(wb_loads(jp, 1))

                pool_products(jp, 1, 2 * (s - 1) + k)

        def finish_weights():
            @pl.when((s == 2) & (uz >= 0) & (uz < U))
            def _():
                j, h, u2 = lax.div(uz, 2), lax.rem(uz, 2), lax.rem(uz, 2)
                for t in range(2):
                    w_copy(uz, t, NEAR).wait_recv()
                    w_copy(uz, t, KEEP).wait_recv()
                    w_copy(uz, t, KEEP).wait_send()
                    both = wkeep[u2, t, 1].astype(F32) + wrecv[u2, t, NEAR].astype(F32)
                    both = both + wrecv[u2, t, KEEP].astype(F32)

                    @pl.when(h == 0)
                    def _():
                        @pl.when(j >= 1)
                        def _():
                            wait_all(wout_stores(j, t))

                        wout[t, 0] = both

                    @pl.when(h == 1)
                    def _():
                        first = wout[t, 0]
                        for k in range(2):
                            wout[t, k] = halves(first, both, k)
                        start_all(wout_stores(j, t))

                @pl.when(uz < U - 2)
                def _():
                    signal(wcredit.at[0], rows=xp)
                    signal(wcredit.at[1], rows=yp)

            @pl.when((s == 3) & (ub >= 0) & (ub < U))
            def _():
                u2 = lax.rem(ub, 2)
                for t in range(2):
                    w_copy(ub, t, FAR).wait_recv()
                    both = wkeep[u2, t, 0].astype(F32) + wrecv[u2, t, FAR].astype(F32)
                    wkeep[u2, t, 0] = both.astype(BF16)
                    w_copy(ub, t, KEEP).start()

        @pl.when((s == 0) & (uz >= 0) & (uz < U))
        def _():
            for t in range(2):
                for kind in (FAR, NEAR):
                    w_copy(uz, t, kind).wait_send()

        @pl.when((s == 0) & (per >= 5) & (par2 == 1))
        def _():
            start_all(wb_loads(jp, 0))

        flows(0)
        share_waits()
        weight_products(0)
        flows(1)
        pool_piece(0)
        flows(2)
        weight_products(1)
        flows(3)
        pool_piece(1)
        flows(4)
        partial_products()
        finish_weights()

        @pl.when((per_m >= 1) & (per_m < U) & (par_m == 1))
        def _():
            part_copy(0, s_m, 0).wait_send()

        for b in range(NS):
            for d in (RIGHT, LEFT):
                shares = (s_m >= 1) if d == LEFT else (s_m >= 0)

                @pl.when(gathers_m & (pos[d] >= s_m))
                def _():
                    @pl.when(pos[d] < L - 1)
                    def _():
                        gath_copy(u_m, p, d, b, s_m, par_m).wait_send()

                    @pl.when(shares)
                    def _():
                        share_copy(u_m, p, c, d, b, s_m, par_m).wait_send()

                @pl.when(sums_m & (pos[d] < s_m))
                def _():
                    sum_copy(ur_m, d, b, s_m, par_m).wait_send()

        @pl.when((s == 2) & (per < SENDING - 1))
        def _():
            @pl.when(has_left)
            def _():
                signal(credit.at[1], feat=f - 2)

            @pl.when(has_right)
            def _():
                signal(credit.at[0], feat=f + 2)

            signal(credit.at[2], feat=sib)

        @pl.when(T == (U + 2) * L + 1)
        def _():
            for j in range(NCH):
                sums_of = [[jnp.sum(sacc[2 * j + h, k], axis=0, keepdims=True) for h in range(2)] for k in range(3)]
                (same, cross, bias) = sums_of
                rows_of = [halves(*same, 0), halves(*cross, 0), halves(*cross, 1), halves(*same, 1)]
                rows_of += [halves(*bias, 0), halves(*bias, 1), jnp.zeros((2, LANE), F32)]
                sred[j] = jnp.concatenate(rows_of, axis=0)
            for k, peer in enumerate((xp, yp, dp)):
                remote(sred.at[peer], srecv.at[k], st_send.at[k], st_recv.at[k], rows=peer).start()

        return carry

    lax.fori_loop(0, TICKS, tick, 0)

    for k, peer in enumerate((xp, yp, dp)):
        copy = remote(sred.at[peer], srecv.at[k], st_send.at[k], st_recv.at[k], rows=peer)
        copy.wait_send()
        copy.wait_recv()
    stats[...] = sred[r] + srecv[0] + srecv[1] + srecv[2]
    for b in range(2):
        wait_all(mix_stores(NCH - 1, b))
    for t in range(2):
        wait_all(wout_stores(NCH - 1, t))
    for i in range(PIECES):
        pg_store(1, i).wait()


def fused(
    pool_a, pool_b, weight_a, weight_b, bias_a, bias_b, stitch, crop_count, row_mask, outgrad_a, outgrad_b
):
    rows, width = pool_a.shape
    chl = bias_a.shape[0]
    NS, L = SUBS, 4
    SB, HB, PB = rows // NS, rows // 2, rows // PIECES
    NCH = chl // LANE
    hbm = pl.BlockSpec(memory_space=pl.ANY)
    vmem = pl.BlockSpec(memory_space=pltpu.VMEM)
    dma = pltpu.SemaphoreType.DMA
    out_shape = (
        jax.ShapeDtypeStruct((rows, chl), BF16),
        jax.ShapeDtypeStruct((rows, chl), BF16),
        jax.ShapeDtypeStruct((rows, width), BF16),
        jax.ShapeDtypeStruct((rows, width), BF16),
        jax.ShapeDtypeStruct((width, 2 * chl), F32),
        jax.ShapeDtypeStruct((width, 2 * chl), F32),
        jax.ShapeDtypeStruct((8, LANE), F32),
    )
    scratch = [
        pltpu.VMEM((2, HB, width), BF16),
        pltpu.VMEM((2, width, rows), BF16),
        pltpu.VMEM((2, width, L * LANE), BF16),
        pltpu.VMEM((L, width, 2 * LANE), BF16),
        pltpu.VMEM((2, L, HB, LANE), BF16),
        pltpu.VMEM((2, 2, L, rows, LANE), BF16),
        pltpu.VMEM((2, 2, L, rows, LANE), BF16),
        pltpu.VMEM((2, 2, 3, rows, LANE), BF16),
        pltpu.VMEM((4, L, 2, rows, LANE), BF16),
        pltpu.VMEM((2, rows, width), F32),
        pltpu.VMEM((2, 2, width, LANE), BF16),
        pltpu.VMEM((2, 2, 2, width, LANE), BF16),
        pltpu.VMEM((2, 2, 3, width, LANE), BF16),
        pltpu.VMEM((2, 2, width, LANE), F32),
        pltpu.VMEM((2, rows, LANE), BF16),
        pltpu.VMEM((rows // LANE, LANE), F32),
        pltpu.VMEM((2 * NCH, 8, LANE), F32),
        pltpu.VMEM((rows, LANE), BF16),
        pltpu.VMEM((2, 2, SB, LANE), BF16),
        pltpu.VMEM((2 * NCH, 3, 8, LANE), F32),
        pltpu.VMEM((NCH, 8, LANE), F32),
        pltpu.VMEM((3, 8, LANE), F32),
        dma((2,)),
        dma((2, L)),
        dma((L, 2)),
        dma((L,)),
        dma((L,)),
        dma((2, NS, L)),
        dma((2, NS, L, 2)),
        dma((2, NS, L)),
        dma((2, NS, L, 2)),
        dma((2, 3)),
        dma((2, 2, 3)),
        dma((2, 2)),
        dma((2,)),
        dma((2, 2)),
        dma((PIECES,)),
        dma((3,)),
        dma((3,)),
        pltpu.SemaphoreType.REGULAR((3,)),
        pltpu.SemaphoreType.REGULAR((2,)),
    ]
    mixed_a, mixed_b, pg_a, pg_b, wg_a, wg_b, stats = pl.pallas_call(
        functools.partial(kernel, rows, width, chl),
        out_shape=out_shape,
        in_specs=[hbm] * 4 + [vmem] * 5 + [hbm] * 2,
        out_specs=(hbm, hbm, hbm, hbm, hbm, hbm, vmem),
        scratch_shapes=scratch,
        compiler_params=pltpu.CompilerParams(
            collective_id=0, has_side_effects=True, vmem_limit_bytes=VMEM_LIMIT
        ),
    )(
        pool_a,
        pool_b,
        weight_a,
        weight_b,
        bias_a[None],
        bias_b[None],
        stitch.reshape(4, chl),
        row_mask[None],
        crop_count[None],
        outgrad_a,
        outgrad_b,
    )
    return mixed_a, mixed_b, pg_a, pg_b, wg_a, wg_b, stats[4], stats[5], stats[:4].reshape(2, 2, LANE)


VMEM_LIMIT = 63 * 1024 * 1024


def plain(
    pool_a, pool_b, weight_a, weight_b, bias_a, bias_b, stitch, crop_count, row_mask, outgrad_a, outgrad_b
):
    row = (row_mask.astype(F32) / crop_count.astype(F32))[:, None]

    def pre(pool, weight, bias):
        partial = dot(pool, weight).astype(BF16)
        return lax.psum_scatter(partial, "feat", scatter_dimension=1, tiled=True).astype(F32) + bias

    def gelu(v):
        cdf = 0.5 * (1.0 + lax.erf(v * INV_SQRT2))
        return v * cdf, cdf + v * (INV_SQRT_2PI * jnp.exp(-0.5 * v * v))

    act_a, slope_a = gelu(pre(pool_a, weight_a, bias_a))
    act_b, slope_b = gelu(pre(pool_b, weight_b, bias_b))
    (s00, s01), (s10, s11) = stitch[0], stitch[1]
    mixed_a = (row * (s00 * act_a + s01 * act_b)).astype(BF16)
    mixed_b = (row * (s10 * act_a + s11 * act_b)).astype(BF16)
    gy_a = row * outgrad_a.astype(F32)
    gy_b = row * outgrad_b.astype(F32)
    gpre_a = ((s00 * gy_a + s10 * gy_b) * slope_a).astype(BF16)
    gpre_b = ((s01 * gy_a + s11 * gy_b) * slope_b).astype(BF16)
    sums = jnp.stack(
        [
            jnp.sum(v, axis=0)
            for v in (
                gy_a * act_a,
                gy_a * act_b,
                gy_b * act_a,
                gy_b * act_b,
                gpre_a.astype(F32),
                gpre_b.astype(F32),
            )
        ]
    )
    sums = lax.psum_scatter(sums, "rows", scatter_dimension=1, tiled=True)

    def back(pool, weight, gpre):
        whole = lax.all_gather(gpre, "feat", axis=1, tiled=True)
        pool_grad = dot_t(whole, weight).astype(BF16)
        wgrad = lax.dot_general(pool, whole, (((0,), (0,)), ((), ())), preferred_element_type=F32)
        wgrad = lax.psum_scatter(wgrad.astype(BF16), "rows", scatter_dimension=1, tiled=True)
        return pool_grad, wgrad.astype(F32)

    pg_a, wg_a = back(pool_a, weight_a, gpre_a)
    pg_b, wg_b = back(pool_b, weight_b, gpre_b)
    return mixed_a, mixed_b, pg_a, pg_b, wg_a, wg_b, sums[4], sums[5], sums[:4].reshape(2, 2, -1)


def shards(
    pool_a, pool_b, weight_a, weight_b, bias_a, bias_b, stitch, crop_count, row_mask, outgrad_a, outgrad_b
):
    rows, width = pool_a.shape
    chl = bias_a.shape[0]
    n_rows, n_feat = lax.axis_size("rows"), lax.axis_size("feat")
    fits = (
        n_rows == 4
        and n_feat == 8
        and chl == n_rows * LANE
        and width % LANE == 0
        and rows % (2 * SUBS * LANE) == 0
    )
    run = fused if fits else plain
    return run(pool_a, pool_b, weight_a, weight_b, bias_a, bias_b, stitch, crop_count, row_mask, outgrad_a, outgrad_b)


def solution(mesh):
    return jax.shard_map(
        shards,
        mesh=mesh,
        in_specs=(
            P("rows", "feat"),
            P("rows", "feat"),
            P("feat", None),
            P("feat", None),
            P("feat"),
            P("feat"),
            P(None, None, "feat"),
            P("rows"),
            P("rows"),
            P("rows", "feat"),
            P("rows", "feat"),
        ),
        out_specs=(
            P("rows", "feat"),
            P("rows", "feat"),
            P("rows", "feat"),
            P("rows", "feat"),
            P("feat", "rows"),
            P("feat", "rows"),
            P(("feat", "rows")),
            P(("feat", "rows")),
            P(None, None, ("feat", "rows")),
        ),
        check_vma=False,
    )
```

time: 328 us -> 316 us (0.963)
  Pallas kernels: 305 us -> 292 us
    pallas_call x1, Pallas kernels: 305 us -> 292 us  [fused(): pl.pallas_call(functools.partial(kernel, rows, width, chl), out_shape=out...]
where the time goes in v3:
time: 316 us; the launch traced here: 315 us
  Pallas kernels  292 us (92%)
  local copies, waits for them, and re-layouts  21.8 us (7%)
    pallas_call x1, Pallas kernels, fused(): pl.pallas_call(functools.partial(kernel, rows, width, chl), out_shape=out...  292 us
    unnamed x18, local copies, waits for them, and re-layouts  15.3 us

profile of v3, /device:TPU:0, one launch (start us, length us, event | category | flops | bytes accessed | tf_op | source)
XLA Modules:
  0.0 315.0 jit_solution(11551631889550018453)
XLA Ops:
  0.6 1.3 broadcast_in_dim.15.refs_8_
  1.9 1.3 broadcast_in_dim.14.refs_7_
  3.2 1.3 reshape.24.refs_6_
  4.5 292.5 %shard_map.178 = (bf16[1280,512]{1,0:T(8,128)(2,1)}, bf16[1280,512]{1,0:T(8,128)(2,1)}, bf16[1280,1152]{1,0:T(8,128)(2,1)}, bf16[1280,1152]{1,0:T(8,128)(2,1)}, ...) custom-call(bf16[1280,1152]{1,0:T(8,128)(2,1)} %refs_0_.1, bf16[1280,1152]{1,0:T(8,128)(2,1)} %refs_1_.1, ...), custom_call_target="tpu_custom_call" | custom-call | tf_op jit(solution)/shard_map/pallas_call | solution.py:697
  297.0 0.0 copy-start.1
  297.0 1.4 slice_bitcast_fusion
  298.4 1.3 slice.11
  299.6 2.5 copy.26
  302.1 0.0 slice-start.2
  302.1 2.6 copy.27
  304.7 0.0 copy-done.1
  304.7 0.0 copy-start
  304.7 0.0 slice-start.3
  304.7 1.6 copy.28
  306.3 1.3 copy-done
  307.6 0.0 slice-start
  307.6 1.6 copy.29
  309.2 0.0 slice-done.2
  309.2 0.0 slice-done.3
  309.2 0.0 slice-start.1
  309.2 2.4 copy.30
  311.6 1.0 slice-done
  312.6 0.2 slice-done.1
  312.8 2.2 copy.31
  (2 shorter events, 0.0 us)
Async XLA Ops:
  297.0 7.7 %copy-start.1 = (bf16[1280,1152]{1,0:T(8,128)(2,1)S(1)}, bf16[1280,1152]{1,0:T(8,128)(2,1)}, u32[]{:S(2)}) copy-start(bf16[1280,1152]{1,0:T(8,128)(2,1)} %get-tuple-element.36) | copy-start | bytes 8847364
  302.1 7.1 %slice-start.2 = ((s8[4718592]{0:T(1024)(128)(4,1)}), s8[4194304]{0:T(1024)(128)(4,1)S(1)}, s32[]{:S(2)}) async-start(s8[4718592]{0:T(1024)(128)(4,1)} %bitcast.9), calls=%async_computation.2 | async-start | bytes 8388608
  304.7 2.9 copy-start
  304.7 4.5 %slice-start.3 = ((s8[4718592]{0:T(1024)(128)(4,1)}), s8[524288]{0:T(1024)(128)(4,1)S(1)}, s32[]{:S(2)}) async-start(s8[4718592]{0:T(1024)(128)(4,1)} %bitcast.9), calls=%async_computation.3 | async-start | bytes 1048576
  307.6 5.0 %slice-start = ((s8[4718592]{0:T(1024)(128)(4,1)}), s8[4194304]{0:T(1024)(128)(4,1)S(1)}, s32[]{:S(2)}) async-start(s8[4718592]{0:T(1024)(128)(4,1)} %bitcast.7), calls=%async_computation | async-start | bytes 8388608
  309.2 3.6 %slice-start.1 = ((s8[4718592]{0:T(1024)(128)(4,1)}), s8[524288]{0:T(1024)(128)(4,1)S(1)}, s32[]{:S(2)}) async-start(s8[4718592]{0:T(1024)(128)(4,1)} %bitcast.7), calls=%async_computation.1 | async-start | bytes 1048576

commit v4 on v3

--- a/solution.py
+++ b/solution.py
@@ -14,6 +14,7 @@
 HALF = 64
 SUBS = 5
 PIECES = 4
+COPIES = 4
 RIGHT, LEFT = 0, 1
 FAR, NEAR, KEEP, OWN = 0, 1, 2, 3
 INV_SQRT2 = 0.7071067811865476
@@ -46,7 +47,7 @@
     (
         pool_a, pool_b, weight_a, weight_b, bias_a, bias_b, stitch, mask, count, og_a, og_b,
         mixed_a, mixed_b, pg_a, pg_b, wg_a, wg_b, stats,
-        pool_v, pool_t, wf, wb, part_sib, part_own, xr, rbuf, gath, acc, wsend, wkeep, wrecv, wout,
+        pool_v, pool_t, wf, wb, part_sib, part_own, xr, rbuf, gath, acc, wsend, wkeep, wrecv, wout_0, wout,
         og_v, scale, par, mix_0, mix_v, sacc, sred, srecv,
         pool_s, wf_s, wb_s, xs_send, xs_recv, z_send, z_recv, g_send, g_recv,
         w_send, w_recv, wout_s, og_s, mix_s, pg_s, st_send, st_recv, credit, wcredit,
@@ -309,8 +310,27 @@
             pg_place(i)[...] = (acc[t, mine, :] + total).astype(BF16)
             pg_store(t, i).start()
 
-    pool_load(0, 0).start()
-    start_all(wf_loads(0, 0))
+    def first_weights(t, other):
+        core = 1 - c if other else c
+        out = []
+        for q in range(L):
+            src = weights[t].at[:, lanes((2 * q + core) * NCH)]
+            if other:
+                tile, k = 2 * t + q // 2, q % 2
+                dst, sem = wb.at[tile, :, k * LANE : (k + 1) * LANE], wb_s.at[tile, k]
+            else:
+                dst, sem = wf.at[t, :, q * LANE : (q + 1) * LANE], wf_s.at[t, q]
+            out.append(pltpu.make_async_copy(src, dst, sem))
+        return out
+
+    def first_rows(t, half):
+        return pltpu.make_async_copy(pools[t].at[half * HB : (half + 1) * HB, :], pool_v.at[t], pool_s.at[t])
+
+    for t in range(2):
+        first_rows(t, 0).start()
+        start_all(first_weights(t, False))
+    for t in range(2):
+        start_all(first_weights(t, True))
 
     bar = pltpu.get_barrier_semaphore()
 
@@ -327,17 +347,41 @@
     signal(bar, rows=yp)
     signal(bar, rows=dp)
     sacc[...] = jnp.zeros_like(sacc)
-    for k in range(rows // LANE):
-        here = slice(k * LANE, (k + 1) * LANE)
-        scale[k : k + 1, :] = mask[:, here].astype(F32) / count[:, here].astype(F32)
+    scale[...] = mask[...].astype(F32) / count[...].astype(F32)
     for u in range(U):
         ch = slice(u // 2 * LANE, (u // 2 + 1) * LANE)
-        s00, s01, s10, s11 = (stitch[k : k + 1, ch] for k in range(4))
+        s00, s01, s10, s11 = (stitch[k // 2, k % 2 : k % 2 + 1, ch] for k in range(4))
         rows_of = (s00, s11), (s01, s10), (s10, s01), (bias_a[:, ch], bias_b[:, ch])
         for k, (one, two) in enumerate(rows_of):
             par[u, k : k + 1, :] = halves(one, two, u % 2)
 
-    pl.semaphore_wait(bar, 4 + has_left.astype(jnp.int32) + has_right.astype(jnp.int32))
+    for half in range(2):
+        here = slice(half * HB, (half + 1) * HB)
+        for t in range(2):
+            first_rows(t, half).wait()
+            if half == 0:
+                wait_all(first_weights(t, False))
+            res = dot(pool_v[t], wf[t]).astype(BF16)
+            for q in range(L):
+                part_own[0, t, q, here, :] = res[:, q * LANE : (q + 1) * LANE]
+        if half == 0:
+            pl.semaphore_wait(bar, 4 + has_left.astype(jnp.int32) + has_right.astype(jnp.int32))
+        for t in range(2):
+            if half == 0:
+                wait_all(first_weights(t, True))
+            else:
+                part_copy(0, t, t).wait_send()
+            for k in range(2):
+                res = dot(pool_v[t], wb[2 * t + k]).astype(BF16)
+                for q in range(2):
+                    part_sib[t, 2 * k + q] = res[:, q * LANE : (q + 1) * LANE]
+            part_copy(0, 2 * half + t, t).start()
+            if half == 0:
+                first_rows(t, 1).start()
+            elif t == 0:
+                pool_load(2 * L, 0).start()
+                start_all(wf_loads(2 * L, 0))
+    part_copy(0, 2, 0).wait_send()
 
     def tick(T, carry):
         per, s = lax.div(T, L), lax.rem(T, L)
@@ -347,7 +391,7 @@
         gathers = (u >= 0) & (u < U)
         sums = (ur >= 0) & (ur < U)
 
-        @pl.when((s == 0) & (per >= 1) & (per < SENDING))
+        @pl.when((s == 0) & (per >= 3) & (per < SENDING))
         def _():
             @pl.when(has_left)
             def _():
@@ -455,7 +499,7 @@
                         part_sib[slot, q] = res[:, q * LANE : (q + 1) * LANE]
                     part_copy(j, s, slot).start()
 
-                @pl.when(per == 0)
+                @pl.when(per == 2)
                 def _():
                     pool_t[t, :, some_rows(half, HB)] = pool_v[slot].T
 
@@ -472,7 +516,7 @@
                 res = row_products(ub, t, dp, first_partner[t])
                 for kind in (FAR, NEAR):
                     wsend[t, kind] = res[:, kind * LANE : (kind + 1) * LANE]
-                    w_copy(ub, t, kind).start()
+                w_copy(ub, t, FAR).start()
 
             @pl.when((s == 1) & (ub >= 0) & (ub < U))
             def _():
@@ -505,6 +549,12 @@
                         wait_all(wb_loads(jp, 1))
 
                 pool_products(jp, 1, 2 * (s - 1) + k)
+
+        def send_near():
+            @pl.when((s == 2) & (ub >= 0) & (ub < U))
+            def _():
+                for t in range(2):
+                    w_copy(ub, t, NEAR).start()
 
         def finish_weights():
             @pl.when((s == 2) & (uz >= 0) & (uz < U))
@@ -523,13 +573,12 @@
                         def _():
                             wait_all(wout_stores(j, t))
 
-                        wout[t, 0] = both
+                        wout_0[t] = both
 
                     @pl.when(h == 1)
                     def _():
-                        first = wout[t, 0]
                         for k in range(2):
-                            wout[t, k] = halves(first, both, k)
+                            wout[t, k] = halves(wout_0[t], both, k).astype(BF16)
                         start_all(wout_stores(j, t))
 
                 @pl.when(uz < U - 2)
@@ -562,6 +611,7 @@
         flows(1)
         pool_piece(0)
         flows(2)
+        send_near()
         weight_products(1)
         flows(3)
         pool_piece(1)
@@ -616,7 +666,7 @@
 
         return carry
 
-    lax.fori_loop(0, TICKS, tick, 0)
+    lax.fori_loop(2 * L, TICKS, tick, 0)
 
     for k, peer in enumerate((xp, yp, dp)):
         copy = remote(sred.at[peer], srecv.at[k], st_send.at[k], st_recv.at[k], rows=peer)
@@ -629,6 +679,35 @@
         wait_all(wout_stores(NCH - 1, t))
     for i in range(PIECES):
         pg_store(1, i).wait()
+
+
+def hand_over(*refs):
+    sources, stats, results = refs[:6], refs[6], refs[7:13]
+    bias_a, bias_b, stitch = refs[13:16]
+    low, held, (load_s, store_s) = refs[16:18], refs[18:24], refs[24:]
+    loads, stores, widen = [], [], []
+    for k in (4, 0, 2, 5, 1, 3):
+        n = results[k].shape[0] // COPIES
+        for i in range(COPIES):
+            some = pl.ds(i * n, n)
+            via = low[k - 4] if k >= 4 else held[k]
+            loads.append(pltpu.make_async_copy(sources[k].at[some, :], via.at[some, :], load_s.at[k, i]))
+            stores.append(pltpu.make_async_copy(held[k].at[some, :], results[k].at[some, :], store_s.at[k, i]))
+            widen.append((via, held[k], some) if k >= 4 else None)
+    for copy in loads:
+        copy.start()
+    bias_a[...] = stats[4:5, :]
+    bias_b[...] = stats[5:6, :]
+    stitch[0] = stats[0:2, :]
+    stitch[1] = stats[2:4, :]
+    for load, store, wide in zip(loads, stores, widen, strict=True):
+        load.wait()
+        if wide is not None:
+            src, dst, some = wide
+            dst[some, :] = src[some, :].astype(F32)
+        store.start()
+    for copy in stores:
+        copy.wait()
 
 
 def fused(
@@ -647,10 +726,11 @@
         jax.ShapeDtypeStruct((rows, chl), BF16),
         jax.ShapeDtypeStruct((rows, width), BF16),
         jax.ShapeDtypeStruct((rows, width), BF16),
-        jax.ShapeDtypeStruct((width, 2 * chl), F32),
-        jax.ShapeDtypeStruct((width, 2 * chl), F32),
+        jax.ShapeDtypeStruct((width, 2 * chl), BF16),
+        jax.ShapeDtypeStruct((width, 2 * chl), BF16),
         jax.ShapeDtypeStruct((8, LANE), F32),
     )
+    results = out_shape[:4] + (jax.ShapeDtypeStruct((width, 2 * chl), F32),) * 2
     scratch = [
         pltpu.VMEM((2, HB, width), BF16),
         pltpu.VMEM((2, width, rows), BF16),
@@ -665,7 +745,8 @@
         pltpu.VMEM((2, 2, width, LANE), BF16),
         pltpu.VMEM((2, 2, 2, width, LANE), BF16),
         pltpu.VMEM((2, 2, 3, width, LANE), BF16),
-        pltpu.VMEM((2, 2, width, LANE), F32),
+        pltpu.VMEM((2, width, LANE), F32),
+        pltpu.VMEM((2, 2, width, LANE), BF16),
         pltpu.VMEM((2, rows, LANE), BF16),
         pltpu.VMEM((rows // LANE, LANE), F32),
         pltpu.VMEM((2 * NCH, 8, LANE), F32),
@@ -710,13 +791,26 @@
         weight_b,
         bias_a[None],
         bias_b[None],
-        stitch.reshape(4, chl),
-        row_mask[None],
-        crop_count[None],
+        stitch,
+        row_mask.reshape(rows // LANE, LANE),
+        crop_count.reshape(rows // LANE, LANE),
         outgrad_a,
         outgrad_b,
     )
-    return mixed_a, mixed_b, pg_a, pg_b, wg_a, wg_b, stats[4], stats[5], stats[:4].reshape(2, 2, LANE)
+    outs = pl.pallas_call(
+        hand_over,
+        out_shape=results
+        + (
+            jax.ShapeDtypeStruct((1, LANE), F32),
+            jax.ShapeDtypeStruct((1, LANE), F32),
+            jax.ShapeDtypeStruct((2, 2, LANE), F32),
+        ),
+        in_specs=[hbm] * 6 + [vmem],
+        out_specs=(hbm,) * 6 + (vmem,) * 3,
+        scratch_shapes=[pltpu.VMEM(out.shape, out.dtype) for out in out_shape[4:6] + results] + [dma((6, COPIES))] * 2,
+        compiler_params=pltpu.CompilerParams(vmem_limit_bytes=VMEM_LIMIT),
+    )(mixed_a, mixed_b, pg_a, pg_b, wg_a, wg_b, stats)
+    return (*outs[:6], outs[6][0], outs[7][0], outs[8])
 
 
 VMEM_LIMIT = 63 * 1024 * 1024

time: 316 us -> 300 us (0.949)
  local copies, waits for them, and re-layouts: 21.8 us -> 0 us
  Pallas kernels: 292 us -> 299 us
    unnamed x18 -> x0, local copies, waits for them, and re-layouts: 15.3 us -> none
    pallas_call x0 -> x1, Pallas kernels: none -> 12.5 us  [fused(): pl.pallas_call(hand_over, out_shape=results + (jax.ShapeDtypeStruct((1, L...]
    pallas_call x1, Pallas kernels: 292 us -> 287 us  [fused(): pl.pallas_call(functools.partial(kernel, rows, width, chl), out_shape=out...]
where the time goes in v4:
time: 300 us
  Pallas kernels  299 us (100%)
    pallas_call x1, Pallas kernels, fused(): pl.pallas_call(functools.partial(kernel, rows, width, chl), out_shape=out...  287 us
    pallas_call x1, Pallas kernels, fused(): pl.pallas_call(hand_over, out_shape=results + (jax.ShapeDtypeStruct((1, L...  12.5 us

profile of v4, /device:TPU:0, one launch (start us, length us, event | category | flops | bytes accessed | tf_op | source)
XLA Modules:
  0.0 299.9 jit_solution(9015315912078594337)
XLA Ops:
  0.6 286.5 %shard_map.178 = (bf16[1280,512]{1,0:T(8,128)(2,1)}, bf16[1280,512]{1,0:T(8,128)(2,1)}, bf16[1280,1152]{1,0:T(8,128)(2,1)}, bf16[1280,1152]{1,0:T(8,128)(2,1)}, ...) custom-call(bf16[1280,1152]{1,0:T(8,128)(2,1)} %refs_0_.1, bf16[1280,1152]{1,0:T(8,128)(2,1)} %refs_1_.1, ...), custom_call_target="tpu_custom_call" | custom-call | tf_op jit(solution)/shard_map/pallas_call | solution.py:778
  287.2 12.5 %shard_map.179 = (bf16[1280,512]{1,0:T(8,128)(2,1)}, bf16[1280,512]{1,0:T(8,128)(2,1)}, bf16[1280,1152]{1,0:T(8,128)(2,1)}, bf16[1280,1152]{1,0:T(8,128)(2,1)}, ...) custom-call(bf16[1280,512]{1,0:T(8,128)(2,1)} %get-tuple-element.25., ...), custom_call_target="tpu_custom_call" | custom-call | tf_op jit(solution)/shard_map/pallas_call | solution.py:800

commit v5 on v4

--- a/solution.py
+++ b/solution.py
@@ -47,15 +47,15 @@
     (
         pool_a, pool_b, weight_a, weight_b, bias_a, bias_b, stitch, mask, count, og_a, og_b,
         mixed_a, mixed_b, pg_a, pg_b, wg_a, wg_b, stats,
-        pool_v, pool_t, wf, wb, part_sib, part_own, xr, rbuf, gath, acc, wsend, wkeep, wrecv, wout_0, wout,
+        pool_0, pool_1, pool_t, wf, wb, part_0, part_1, part_own, xr, rbuf, gath, acc, wsend, wkeep, wrecv, wout_0, wout,
         og_v, scale, par, mix_0, mix_v, sacc, sred, srecv,
-        pool_s, wf_s, wb_s, xs_send, xs_recv, z_send, z_recv, g_send, g_recv,
+        pool_s, wf_s, wb_s, xs_send, xs_recv, x0_send, x0_recv, z_send, z_recv, g_send, g_recv,
         w_send, w_recv, wout_s, og_s, mix_s, pg_s, st_send, st_recv, credit, wcredit,
     ) = refs
     L = 4
     NS = SUBS
     SB = rows // NS
-    HB = rows // 2
+    BIG, SMALL = rows * 3 // 10, rows // 5
     PB = rows // PIECES
     NCH = chl // LANE
     U = 2 * NCH
@@ -110,21 +110,27 @@
             def _():
                 run(t)
 
-    def pool_load(tick, t):
-        slot = lax.rem(tick, 2)
-        half = lax.div(lax.rem(tick, L), 2)
-        return pltpu.make_async_copy(pools[t].at[some_rows(half, HB), :], pool_v.at[slot], pool_s.at[slot])
-
-    def wf_loads(tick, t):
-        j = lax.div(tick, 2 * L)
-        slot = lax.rem(tick, 2)
-        core = jnp.where(lax.rem(lax.div(tick, L), 2) == 0, c, 1 - c)
+    sizes, pool_v, part_v = (BIG, SMALL), (pool_0, pool_1), (part_0, part_1)
+
+    def piece_rows(s, k):
+        return pl.ds(pl.multiple_of(lax.div(s, 2) * (BIG + SMALL) + k * BIG, LANE), sizes[k])
+
+    def pool_loads(s, k):
+        return [
+            pltpu.make_async_copy(pools[t].at[piece_rows(s, k), :], pool_v[k].at[t], pool_s.at[k, t])
+            for t in range(2)
+        ]
+
+    def wf_loads(per):
+        j = lax.div(per, 2)
+        core = jnp.where(lax.rem(per, 2) == 0, c, 1 - c)
         return [
             pltpu.make_async_copy(
                 weights[t].at[:, lanes((2 * q + core) * NCH + j)],
-                wf.at[slot, :, q * LANE : (q + 1) * LANE],
-                wf_s.at[slot, q],
+                wf.at[t, :, q * LANE : (q + 1) * LANE],
+                wf_s.at[t, q],
             )
+            for t in range(2)
             for q in range(L)
         ]
 
@@ -150,13 +156,21 @@
             for t in range(2)
         ]
 
-    def part_copy(j, s, slot):
-        t, half = lax.rem(s, 2), lax.div(s, 2)
+    def part_copy(j, s, k):
         return remote(
-            part_sib.at[slot],
-            xr.at[lax.rem(j, 2), t, :, some_rows(half, HB), :],
+            part_v[k],
+            xr.at[lax.rem(j, 2), :, :, piece_rows(s, k), :],
             xs_send.at[s],
             xs_recv.at[s],
+            feat=sib,
+        )
+
+    def first_copy(h, s, k):
+        return remote(
+            part_v[k].at[lax.div(s, 2)],
+            xr.at[0, h, :, piece_rows(s, k), :],
+            x0_send.at[h, s],
+            x0_recv.at[h, s],
             feat=sib,
         )
 
@@ -188,13 +202,8 @@
         return jnp.where(upper(one.shape[0]) == (h == 1), one, swap(two))
 
     def own_sum(u, o, b):
-        j, h = lax.div(u, 2), lax.rem(u, 2)
-        j2 = lax.rem(j, 2)
-
-        def tower(t):
-            return part_own[j2, t, o, sub_rows(b), :].astype(F32) + xr[j2, t, o, sub_rows(b), :].astype(F32)
-
-        return packed(tower(h), tower(1 - h), h)
+        h, j2 = lax.rem(u, 2), lax.rem(lax.div(u, 2), 2)
+        return part_own[j2, h, o, sub_rows(b), :].astype(F32) + xr[j2, h, o, sub_rows(b), :].astype(F32)
 
     def fold(v):
         return jnp.sum(v.reshape(SB // 8, 8, LANE), axis=0)
@@ -271,11 +280,9 @@
             for k in range(2)
         ]
 
-    def pg_place(i):
-        return pool_v.at[lax.div(i, 2), some_rows(lax.rem(i, 2), PB), :]
-
     def pg_store(t, i):
-        return pltpu.make_async_copy(pg_place(i), pgs[t].at[some_rows(i, PB), :], pg_s.at[i])
+        place = pool_0.at[lax.rem(i, 2), pl.ds(0, PB), :]
+        return pltpu.make_async_copy(place, pgs[t].at[some_rows(i, PB), :], pg_s.at[lax.rem(i, 2)])
 
     def row_products(u, t, one, two):
         cols = []
@@ -307,30 +314,32 @@
         def _():
             if t > 0:
                 pg_store(t, i).wait()
-            pg_place(i)[...] = (acc[t, mine, :] + total).astype(BF16)
+            else:
+
+                @pl.when(i >= 2)
+                def _():
+                    pg_store(t, i).wait()
+
+            pool_0[lax.rem(i, 2), pl.ds(0, PB), :] = (acc[t, mine, :] + total).astype(BF16)
             pg_store(t, i).start()
 
-    def first_weights(t, other):
-        core = 1 - c if other else c
-        out = []
-        for q in range(L):
-            src = weights[t].at[:, lanes((2 * q + core) * NCH)]
-            if other:
+    def first_weights():
+        out = wf_loads(0)
+        for t in range(2):
+            for q in range(L):
                 tile, k = 2 * t + q // 2, q % 2
-                dst, sem = wb.at[tile, :, k * LANE : (k + 1) * LANE], wb_s.at[tile, k]
-            else:
-                dst, sem = wf.at[t, :, q * LANE : (q + 1) * LANE], wf_s.at[t, q]
-            out.append(pltpu.make_async_copy(src, dst, sem))
+                out.append(
+                    pltpu.make_async_copy(
+                        weights[t].at[:, lanes((2 * q + 1 - c) * NCH)],
+                        wb.at[tile, :, k * LANE : (k + 1) * LANE],
+                        wb_s.at[tile, k],
+                    )
+                )
         return out
 
-    def first_rows(t, half):
-        return pltpu.make_async_copy(pools[t].at[half * HB : (half + 1) * HB, :], pool_v.at[t], pool_s.at[t])
-
-    for t in range(2):
-        first_rows(t, 0).start()
-        start_all(first_weights(t, False))
-    for t in range(2):
-        start_all(first_weights(t, True))
+    start_all(first_weights())
+    start_all(pool_loads(0, 0))
+    start_all(pool_loads(1, 1))
 
     bar = pltpu.get_barrier_semaphore()
 
@@ -355,33 +364,44 @@
         for k, (one, two) in enumerate(rows_of):
             par[u, k : k + 1, :] = halves(one, two, u % 2)
 
-    for half in range(2):
-        here = slice(half * HB, (half + 1) * HB)
+    def first_tiles(h):
         for t in range(2):
-            first_rows(t, half).wait()
-            if half == 0:
-                wait_all(first_weights(t, False))
-            res = dot(pool_v[t], wf[t]).astype(BF16)
             for q in range(L):
-                part_own[0, t, q, here, :] = res[:, q * LANE : (q + 1) * LANE]
-        if half == 0:
+                mine = wf[t, :, q * LANE : (q + 1) * LANE]
+                other = wb[2 * t + q // 2, :, q % 2 * LANE : (q % 2 + 1) * LANE]
+                gath[3 - h, q, t, :width, :] = halves(mine, other, h)
+
+    def first_products(h, s, k, slot):
+        res = []
+        for t in range(2):
+            cols = jnp.concatenate([gath[3 - h, q, t, :width, :] for q in range(L)], axis=1)
+            res.append(dot(pool_v[k][t], cols).astype(BF16))
+        for q in range(L):
+            both = [v[:, q * LANE : (q + 1) * LANE] for v in res]
+            part_own[0, h, q, piece_rows(s, k), :] = halves(*both, 0)
+            part_v[k][slot, q] = halves(*both, 1)
+
+    wait_all(first_weights())
+    first_tiles(0)
+    for s in range(L):
+        k = s % 2
+        wait_all(pool_loads(s, k))
+        first_products(0, s, k, s // 2)
+        if s < 3:
+            start_all(pool_loads((s + 2) % L, k))
+        if s == 0:
             pl.semaphore_wait(bar, 4 + has_left.astype(jnp.int32) + has_right.astype(jnp.int32))
-        for t in range(2):
-            if half == 0:
-                wait_all(first_weights(t, True))
-            else:
-                part_copy(0, t, t).wait_send()
-            for k in range(2):
-                res = dot(pool_v[t], wb[2 * t + k]).astype(BF16)
-                for q in range(2):
-                    part_sib[t, 2 * k + q] = res[:, q * LANE : (q + 1) * LANE]
-            part_copy(0, 2 * half + t, t).start()
-            if half == 0:
-                first_rows(t, 1).start()
-            elif t == 0:
-                pool_load(2 * L, 0).start()
-                start_all(wf_loads(2 * L, 0))
-    part_copy(0, 2, 0).wait_send()
+        first_copy(0, s, k).start()
+    first_tiles(1)
+    start_all(wf_loads(2))
+    for s in range(L):
+        first_copy(0, s, s % 2).wait_recv()
+    for d in (RIGHT, LEFT):
+        @pl.when(pos[d] == 0)
+        def _():
+            for b in range(NS):
+                sum_block(0, d, b, 0)[...] = own_sum(0, p + (L - 1) * (1 - 2 * d), b).astype(BF16)
+                sum_copy(0, d, b, 1, 0).start()
 
     def tick(T, carry):
         per, s = lax.div(T, L), lax.rem(T, L)
@@ -405,9 +425,17 @@
 
         @pl.when((s == 1) & sums & (par2 == 0))
         def _():
+            @pl.when(ur > 0)
+            def _():
+                for k in range(L):
+                    part_copy(lax.div(ur, 2), k, k % 2).wait_recv()
+
+            start_all(og_loads(lax.div(ur, 2)))
+
+        @pl.when(T == 3 * L + 1)
+        def _():
             for k in range(L):
-                part_copy(lax.div(ur, 2), k, 0).wait_recv()
-            start_all(og_loads(lax.div(ur, 2)))
+                first_copy(1, k, k % 2).wait_recv()
 
         before = T - 1 + L
         per_m, s_m = lax.div(before, L) - 1, lax.rem(before, L)
@@ -444,7 +472,9 @@
                     def _():
                         share_copy(u, o, c, d, b, s, par2).start()
 
-                @pl.when(sums & jnp.logical_not(gather_here))
+                begun = (ur == 0) & (s == 1)
+
+                @pl.when(sums & jnp.logical_not(gather_here | begun))
                 def _():
                     block = sum_block(ur, d, b, s - 1)
 
@@ -472,36 +502,58 @@
         def partial_products():
             @pl.when(per < U)
             def _():
-                slot = lax.rem(T, 2)
-                pool_load(T, 0).wait()
-                wait_all(wf_loads(T, 0))
-
-                @pl.when(T + 1 < U * L)
+                @pl.when(s == 0)
                 def _():
-                    def load(t):
-                        pool_load(T + 1, t).start()
-                        start_all(wf_loads(T + 1, t))
-
-                    tower_of(T + 1, load)
+                    wait_all(wf_loads(per))
 
                 j = lax.div(per, 2)
-                t, half = lax.rem(s, 2), lax.div(s, 2)
-                res = dot(pool_v[slot], wf[slot]).astype(BF16)
-
-                @pl.when(par2 == 0)
+                for k in range(2):
+
+                    @pl.when(lax.rem(s, 2) == k)
+                    def _():
+                        wait_all(pool_loads(s, k))
+
+                        @pl.when(per == 2)
+                        def _():
+                            first_copy(0, s, k).wait_send()
+                            first_products(1, s, k, lax.div(s, 2))
+                            first_copy(1, s, k).start()
+
+                        @pl.when((per == 3) & (s < 2))
+                        def _():
+                            for i in range(2):
+                                first_copy(1, s + 2 * i, k).wait_send()
+
+                        @pl.when(T + 1 < U * L)
+                        def _():
+                            start_all(pool_loads(lax.rem(s + 1, L), 1 - k))
+
+                        res = [dot(pool_v[k][t], wf[t]).astype(BF16) for t in range(2)]
+                        for q in range(L):
+                            both = [v[:, q * LANE : (q + 1) * LANE] for v in res]
+                            for h in range(2):
+                                block = halves(*both, h)
+
+                                @pl.when(par2 == 0)
+                                def _():
+                                    part_own[lax.rem(j, 2), h, q, piece_rows(s, k), :] = block
+
+                                @pl.when(par2 == 1)
+                                def _():
+                                    part_v[k][h, q] = block
+
+                        @pl.when(par2 == 1)
+                        def _():
+                            part_copy(j, s, k).start()
+
+                        @pl.when(per == 2)
+                        def _():
+                            for t in range(2):
+                                pool_t[t, :, piece_rows(s, k)] = pool_v[k][t].T
+
+                @pl.when((s == L - 1) & (per + 1 < U))
                 def _():
-                    for q in range(L):
-                        part_own[lax.rem(j, 2), t, q, some_rows(half, HB), :] = res[:, q * LANE : (q + 1) * LANE]
-
-                @pl.when(par2 == 1)
-                def _():
-                    for q in range(L):
-                        part_sib[slot, q] = res[:, q * LANE : (q + 1) * LANE]
-                    part_copy(j, s, slot).start()
-
-                @pl.when(per == 2)
-                def _():
-                    pool_t[t, :, some_rows(half, HB)] = pool_v[slot].T
+                    start_all(wf_loads(per + 1))
 
         def weight_products(t):
             @pl.when((s == 0) & (ub >= 0) & (ub < U))
@@ -619,9 +671,11 @@
         partial_products()
         finish_weights()
 
-        @pl.when((per_m >= 1) & (per_m < U) & (par_m == 1))
-        def _():
-            part_copy(0, s_m, 0).wait_send()
+        for k in range(2):
+
+            @pl.when((per_m >= 3) & (per_m < U) & (par_m == 1) & (lax.rem(s_m, 2) == k))
+            def _():
+                part_copy(0, s_m, k).wait_send()
 
         for b in range(NS):
             for d in (RIGHT, LEFT):
@@ -677,7 +731,7 @@
         wait_all(mix_stores(NCH - 1, b))
     for t in range(2):
         wait_all(wout_stores(NCH - 1, t))
-    for i in range(PIECES):
+    for i in range(2):
         pg_store(1, i).wait()
 
 
@@ -716,7 +770,7 @@
     rows, width = pool_a.shape
     chl = bias_a.shape[0]
     NS, L = SUBS, 4
-    SB, HB, PB = rows // NS, rows // 2, rows // PIECES
+    BIG, SMALL = rows * 3 // 10, rows // 5
     NCH = chl // LANE
     hbm = pl.BlockSpec(memory_space=pl.ANY)
     vmem = pl.BlockSpec(memory_space=pltpu.VMEM)
@@ -732,11 +786,13 @@
     )
     results = out_shape[:4] + (jax.ShapeDtypeStruct((width, 2 * chl), F32),) * 2
     scratch = [
-        pltpu.VMEM((2, HB, width), BF16),
+        pltpu.VMEM((2, BIG, width), BF16),
+        pltpu.VMEM((2, SMALL, width), BF16),
         pltpu.VMEM((2, width, rows), BF16),
         pltpu.VMEM((2, width, L * LANE), BF16),
         pltpu.VMEM((L, width, 2 * LANE), BF16),
-        pltpu.VMEM((2, L, HB, LANE), BF16),
+        pltpu.VMEM((2, L, BIG, LANE), BF16),
+        pltpu.VMEM((2, L, SMALL, LANE), BF16),
         pltpu.VMEM((2, 2, L, rows, LANE), BF16),
         pltpu.VMEM((2, 2, L, rows, LANE), BF16),
         pltpu.VMEM((2, 2, 3, rows, LANE), BF16),
@@ -751,15 +807,17 @@
         pltpu.VMEM((rows // LANE, LANE), F32),
         pltpu.VMEM((2 * NCH, 8, LANE), F32),
         pltpu.VMEM((rows, LANE), BF16),
-        pltpu.VMEM((2, 2, SB, LANE), BF16),
+        pltpu.VMEM((2, 2, rows // NS, LANE), BF16),
         pltpu.VMEM((2 * NCH, 3, 8, LANE), F32),
         pltpu.VMEM((NCH, 8, LANE), F32),
         pltpu.VMEM((3, 8, LANE), F32),
-        dma((2,)),
+        dma((2, 2)),
         dma((2, L)),
         dma((L, 2)),
         dma((L,)),
         dma((L,)),
+        dma((2, L)),
+        dma((2, L)),
         dma((2, NS, L)),
         dma((2, NS, L, 2)),
         dma((2, NS, L)),
@@ -769,7 +827,7 @@
         dma((2, 2)),
         dma((2,)),
         dma((2, 2)),
-        dma((PIECES,)),
+        dma((2,)),
         dma((3,)),
         dma((3,)),
         pltpu.SemaphoreType.REGULAR((3,)),
@@ -876,6 +934,7 @@
         and n_feat == 8
         and chl == n_rows * LANE
         and width % LANE == 0
+        and width <= rows
         and rows % (2 * SUBS * LANE) == 0
     )
     run = fused if fits else plain

time: 300 us -> 299 us (level)
  no operation moved by 1% of the time
where the time goes in v5:
time: 299 us
  Pallas kernels  298 us (100%)
    pallas_call x1, Pallas kernels, fused(): pl.pallas_call(functools.partial(kernel, rows, width, chl), out_shape=out...  285 us
    pallas_call x1, Pallas kernels, fused(): pl.pallas_call(hand_over, out_shape=results + (jax.ShapeDtypeStruct((1, L...  12.5 us

profile of v5, /device:TPU:0, one launch (start us, length us, event | category | flops | bytes accessed | tf_op | source)
XLA Modules:
  0.0 298.6 jit_solution(5657224095261472784)
XLA Ops:
  0.6 285.3 %shard_map.178 = (bf16[1280,512]{1,0:T(8,128)(2,1)}, bf16[1280,512]{1,0:T(8,128)(2,1)}, bf16[1280,1152]{1,0:T(8,128)(2,1)}, bf16[1280,1152]{1,0:T(8,128)(2,1)}, ...) custom-call(bf16[1280,1152]{1,0:T(8,128)(2,1)} %refs_0_.1, bf16[1280,1152]{1,0:T(8,128)(2,1)} %refs_1_.1, ...), custom_call_target="tpu_custom_call" | custom-call | tf_op jit(solution)/shard_map/pallas_call | solution.py:836
  285.9 12.5 %shard_map.179 = (bf16[1280,512]{1,0:T(8,128)(2,1)}, bf16[1280,512]{1,0:T(8,128)(2,1)}, bf16[1280,1152]{1,0:T(8,128)(2,1)}, bf16[1280,1152]{1,0:T(8,128)(2,1)}, ...) custom-call(bf16[1280,512]{1,0:T(8,128)(2,1)} %get-tuple-element.25., ...), custom_call_target="tpu_custom_call" | custom-call | tf_op jit(solution)/shard_map/pallas_call | solution.py:858

commit v6 on v5

--- a/solution.py
+++ b/solution.py
@@ -46,11 +46,11 @@
 def kernel(rows, width, chl, *refs):
     (
         pool_a, pool_b, weight_a, weight_b, bias_a, bias_b, stitch, mask, count, og_a, og_b,
-        mixed_a, mixed_b, pg_a, pg_b, wg_a, wg_b, stats,
-        pool_0, pool_1, pool_t, wf, wb, part_0, part_1, part_own, xr, rbuf, gath, acc, wsend, wkeep, wrecv, wout_0, wout,
+        mixed_a, mixed_b, acc, wg_a, wg_b, stats,
+        pool_0, pool_1, pool_t, wf, wb, part_0, part_1, part_own, xr, rbuf, gath, wsend, wkeep, wrecv, wout_0, wout,
         og_v, scale, par, mix_0, mix_v, sacc, sred, srecv,
         pool_s, wf_s, wb_s, xs_send, xs_recv, x0_send, x0_recv, z_send, z_recv, g_send, g_recv,
-        w_send, w_recv, wout_s, og_s, mix_s, pg_s, st_send, st_recv, credit, wcredit,
+        w_send, w_recv, wout_s, og_s, mix_s, st_send, st_recv, credit, wcredit,
     ) = refs
     L = 4
     NS = SUBS
@@ -63,7 +63,7 @@
     TICKS = (U + 5) * L
     pools, weights = (pool_a, pool_b), (weight_a, weight_b)
     ogs, mixeds = (og_a, og_b), (mixed_a, mixed_b)
-    pgs, wgs = (pg_a, pg_b), (wg_a, wg_b)
+    wgs = (wg_a, wg_b)
 
     f = lax.axis_index("feat")
     r = lax.axis_index("rows")
@@ -280,10 +280,6 @@
             for k in range(2)
         ]
 
-    def pg_store(t, i):
-        place = pool_0.at[lax.rem(i, 2), pl.ds(0, PB), :]
-        return pltpu.make_async_copy(place, pgs[t].at[some_rows(i, PB), :], pg_s.at[lax.rem(i, 2)])
-
     def row_products(u, t, one, two):
         cols = []
         for owner in (one, two):
@@ -306,22 +302,9 @@
         def _():
             acc[t, mine, :] = total
 
-        @pl.when((j > 0) & (j < NCH - 1))
+        @pl.when(j > 0)
         def _():
             acc[t, mine, :] += total
-
-        @pl.when(j == NCH - 1)
-        def _():
-            if t > 0:
-                pg_store(t, i).wait()
-            else:
-
-                @pl.when(i >= 2)
-                def _():
-                    pg_store(t, i).wait()
-
-            pool_0[lax.rem(i, 2), pl.ds(0, PB), :] = (acc[t, mine, :] + total).astype(BF16)
-            pg_store(t, i).start()
 
     def first_weights():
         out = wf_loads(0)
@@ -394,14 +377,17 @@
         first_copy(0, s, k).start()
     first_tiles(1)
     start_all(wf_loads(2))
-    for s in range(L):
-        first_copy(0, s, s % 2).wait_recv()
-    for d in (RIGHT, LEFT):
-        @pl.when(pos[d] == 0)
-        def _():
-            for b in range(NS):
-                sum_block(0, d, b, 0)[...] = own_sum(0, p + (L - 1) * (1 - 2 * d), b).astype(BF16)
-                sum_copy(0, d, b, 1, 0).start()
+
+    def begin_sums():
+        for i in range(L):
+            first_copy(0, i, i % 2).wait_recv()
+        for d in (RIGHT, LEFT):
+
+            @pl.when(pos[d] == 0)
+            def _():
+                for b in range(NS):
+                    sum_block(0, d, b, 0)[...] = own_sum(0, p + (L - 1) * (1 - 2 * d), b).astype(BF16)
+                    sum_copy(0, d, b, 1, 0).start()
 
     def tick(T, carry):
         per, s = lax.div(T, L), lax.rem(T, L)
@@ -502,10 +488,6 @@
         def partial_products():
             @pl.when(per < U)
             def _():
-                @pl.when(s == 0)
-                def _():
-                    wait_all(wf_loads(per))
-
                 j = lax.div(per, 2)
                 for k in range(2):
 
@@ -518,6 +500,17 @@
                             first_copy(0, s, k).wait_send()
                             first_products(1, s, k, lax.div(s, 2))
                             first_copy(1, s, k).start()
+                            if k == 0:
+
+                                @pl.when(s == 0)
+                                def _():
+                                    begin_sums()
+
+                        if k == 0:
+
+                            @pl.when(s == 0)
+                            def _():
+                                wait_all(wf_loads(per))
 
                         @pl.when((per == 3) & (s < 2))
                         def _():
@@ -546,7 +539,7 @@
                         def _():
                             part_copy(j, s, k).start()
 
-                        @pl.when(per == 2)
+                        @pl.when(per == 3)
                         def _():
                             for t in range(2):
                                 pool_t[t, :, piece_rows(s, k)] = pool_v[k][t].T
@@ -731,37 +724,40 @@
         wait_all(mix_stores(NCH - 1, b))
     for t in range(2):
         wait_all(wout_stores(NCH - 1, t))
-    for i in range(2):
-        pg_store(1, i).wait()
-
-
-def hand_over(*refs):
-    sources, stats, results = refs[:6], refs[6], refs[7:13]
-    bias_a, bias_b, stitch = refs[13:16]
-    low, held, (load_s, store_s) = refs[16:18], refs[18:24], refs[24:]
-    loads, stores, widen = [], [], []
-    for k in (4, 0, 2, 5, 1, 3):
+
+
+def hand_over(mixed_a, mixed_b, acc, wg_a, wg_b, stats, *refs):
+    results, (bias_a, bias_b, stitch) = refs[:6], refs[6:9]
+    low, held, (load_s, store_s) = refs[9:11], refs[11:17], refs[17:]
+    sources = {0: mixed_a, 1: mixed_b, 4: wg_a, 5: wg_b}
+    steps = []
+    for k in (4, 0, 5, 1, 2, 3):
         n = results[k].shape[0] // COPIES
         for i in range(COPIES):
             some = pl.ds(i * n, n)
-            via = low[k - 4] if k >= 4 else held[k]
-            loads.append(pltpu.make_async_copy(sources[k].at[some, :], via.at[some, :], load_s.at[k, i]))
-            stores.append(pltpu.make_async_copy(held[k].at[some, :], results[k].at[some, :], store_s.at[k, i]))
-            widen.append((via, held[k], some) if k >= 4 else None)
-    for copy in loads:
-        copy.start()
+            load = None
+            if k in sources:
+                via = low[k - 4] if k >= 4 else held[k]
+                load = pltpu.make_async_copy(sources[k].at[some, :], via.at[some, :], load_s.at[k, i])
+            store = pltpu.make_async_copy(held[k].at[some, :], results[k].at[some, :], store_s.at[k, i])
+            steps.append((k, some, load, store))
+    for _, _, load, _ in steps:
+        if load is not None:
+            load.start()
     bias_a[...] = stats[4:5, :]
     bias_b[...] = stats[5:6, :]
     stitch[0] = stats[0:2, :]
     stitch[1] = stats[2:4, :]
-    for load, store, wide in zip(loads, stores, widen, strict=True):
-        load.wait()
-        if wide is not None:
-            src, dst, some = wide
-            dst[some, :] = src[some, :].astype(F32)
+    for k, some, load, store in sorted(steps, key=lambda step: (2, 3, 4, 0, 5, 1).index(step[0])):
+        if load is not None:
+            load.wait()
+        if k >= 4:
+            held[k][some, :] = low[k - 4][some, :].astype(F32)
+        elif k >= 2:
+            held[k][some, :] = acc[k - 2, some, :].astype(BF16)
         store.start()
-    for copy in stores:
-        copy.wait()
+    for _, _, _, store in steps:
+        store.wait()
 
 
 def fused(
@@ -778,13 +774,16 @@
     out_shape = (
         jax.ShapeDtypeStruct((rows, chl), BF16),
         jax.ShapeDtypeStruct((rows, chl), BF16),
-        jax.ShapeDtypeStruct((rows, width), BF16),
-        jax.ShapeDtypeStruct((rows, width), BF16),
+        pltpu.VMEM((2, rows, width), F32),
         jax.ShapeDtypeStruct((width, 2 * chl), BF16),
         jax.ShapeDtypeStruct((width, 2 * chl), BF16),
         jax.ShapeDtypeStruct((8, LANE), F32),
     )
-    results = out_shape[:4] + (jax.ShapeDtypeStruct((width, 2 * chl), F32),) * 2
+    results = (
+        out_shape[:2]
+        + (jax.ShapeDtypeStruct((rows, width), BF16),) * 2
+        + (jax.ShapeDtypeStruct((width, 2 * chl), F32),) * 2
+    )
     scratch = [
         pltpu.VMEM((2, BIG, width), BF16),
         pltpu.VMEM((2, SMALL, width), BF16),
@@ -797,7 +796,6 @@
         pltpu.VMEM((2, 2, L, rows, LANE), BF16),
         pltpu.VMEM((2, 2, 3, rows, LANE), BF16),
         pltpu.VMEM((4, L, 2, rows, LANE), BF16),
-        pltpu.VMEM((2, rows, width), F32),
         pltpu.VMEM((2, 2, width, LANE), BF16),
         pltpu.VMEM((2, 2, 2, width, LANE), BF16),
         pltpu.VMEM((2, 2, 3, width, LANE), BF16),
@@ -827,17 +825,16 @@
         dma((2, 2)),
         dma((2,)),
         dma((2, 2)),
-        dma((2,)),
         dma((3,)),
         dma((3,)),
         pltpu.SemaphoreType.REGULAR((3,)),
         pltpu.SemaphoreType.REGULAR((2,)),
     ]
-    mixed_a, mixed_b, pg_a, pg_b, wg_a, wg_b, stats = pl.pallas_call(
+    mixed_a, mixed_b, acc, wg_a, wg_b, stats = pl.pallas_call(
         functools.partial(kernel, rows, width, chl),
         out_shape=out_shape,
         in_specs=[hbm] * 4 + [vmem] * 5 + [hbm] * 2,
-        out_specs=(hbm, hbm, hbm, hbm, hbm, hbm, vmem),
+        out_specs=(hbm, hbm, vmem, hbm, hbm, vmem),
         scratch_shapes=scratch,
         compiler_params=pltpu.CompilerParams(
             collective_id=0, has_side_effects=True, vmem_limit_bytes=VMEM_LIMIT
@@ -855,6 +852,9 @@
         outgrad_a,
         outgrad_b,
     )
+    held = [pltpu.with_memory_space_constraint(v, pltpu.HBM) for v in (mixed_a, mixed_b, acc, wg_a, wg_b)]
+    held[2] = pltpu.with_memory_space_constraint(acc, pltpu.VMEM)
+    held.append(stats)
     outs = pl.pallas_call(
         hand_over,
         out_shape=results
@@ -863,15 +863,15 @@
             jax.ShapeDtypeStruct((1, LANE), F32),
             jax.ShapeDtypeStruct((2, 2, LANE), F32),
         ),
-        in_specs=[hbm] * 6 + [vmem],
+        in_specs=[hbm, hbm, vmem, hbm, hbm, vmem],
         out_specs=(hbm,) * 6 + (vmem,) * 3,
-        scratch_shapes=[pltpu.VMEM(out.shape, out.dtype) for out in out_shape[4:6] + results] + [dma((6, COPIES))] * 2,
+        scratch_shapes=[pltpu.VMEM(out.shape, out.dtype) for out in out_shape[3:5] + results] + [dma((6, COPIES))] * 2,
         compiler_params=pltpu.CompilerParams(vmem_limit_bytes=VMEM_LIMIT),
-    )(mixed_a, mixed_b, pg_a, pg_b, wg_a, wg_b, stats)
+    )(*held)
     return (*outs[:6], outs[6][0], outs[7][0], outs[8])
 
 
-VMEM_LIMIT = 63 * 1024 * 1024
+VMEM_LIMIT = 52 * 1024 * 1024
 
 
 def plain(

time: 299 us -> 296 us (0.990)
  Pallas kernels: 298 us -> 294 us
where the time goes in v6:
time: 296 us; the launch traced here: 295 us
  Pallas kernels  294 us (99%)
    pallas_call x1, Pallas kernels, fused(): pl.pallas_call(functools.partial(kernel, rows, width, chl), out_shape=out...  284 us
    pallas_call x1, Pallas kernels, fused(): pl.pallas_call(hand_over, out_shape=results + (jax.ShapeDtypeStruct((1, L...  10.5 us

profile of v6, /device:TPU:0, one launch (start us, length us, event | category | flops | bytes accessed | tf_op | source)
XLA Modules:
  0.0 295.3 jit_solution(12456602043416987824)
XLA Ops:
  0.6 284.0 %shard_map.178 = (bf16[1280,512]{1,0:T(8,128)(2,1)}, bf16[1280,512]{1,0:T(8,128)(2,1)}, f32[2,1280,1152]{2,1,0:T(8,128)S(1)}, bf16[1152,1024]{1,0:T(8,128)(2,1)}...) custom-call(bf16[1280,1152]{1,0:T(8,128)(2,1)} %refs_0_.1, bf16[1280,1152]{1,0:T(8,128)(2,1)} %refs_1_.1, ...), custom_call_target="tpu_custom_call" | custom-call | tf_op jit(solution)/shard_map/pallas_call | solution.py:833
  284.6 10.5 %shard_map.179 = (bf16[1280,512]{1,0:T(8,128)(2,1)}, bf16[1280,512]{1,0:T(8,128)(2,1)}, bf16[1280,1152]{1,0:T(8,128)(2,1)}, bf16[1280,1152]{1,0:T(8,128)(2,1)}, ...) custom-call(bf16[1280,512]{1,0:T(8,128)(2,1)} %get-tuple-element.24., ...), custom_call_target="tpu_custom_call" | custom-call | tf_op jit(solution)/shard_map/pallas_call | solution.py:858

commit v7 on v6

--- a/solution.py
+++ b/solution.py
@@ -47,10 +47,10 @@
     (
         pool_a, pool_b, weight_a, weight_b, bias_a, bias_b, stitch, mask, count, og_a, og_b,
         mixed_a, mixed_b, acc, wg_a, wg_b, stats,
-        pool_0, pool_1, pool_t, wf, wb, part_0, part_1, part_own, xr, rbuf, gath, wsend, wkeep, wrecv, wout_0, wout,
-        og_v, scale, par, mix_0, mix_v, sacc, sred, srecv,
+        pool_0, pool_1, pool_t, wf, wb, part_0, part_1, part_own, xr, rbuf, gath, wsend, wkeep, wrecv, wout,
+        og_v, scale, par, sacc, sred, srecv,
         pool_s, wf_s, wb_s, xs_send, xs_recv, x0_send, x0_recv, z_send, z_recv, g_send, g_recv,
-        w_send, w_recv, wout_s, og_s, mix_s, st_send, st_recv, credit, wcredit,
+        w_send, w_recv, wout_s, og_s, st_send, st_recv, credit, wcredit,
     ) = refs
     L = 4
     NS = SUBS
@@ -149,12 +149,6 @@
 
     def og_loads(j):
         return [pltpu.make_async_copy(ogs[t].at[:, lanes(j)], og_v.at[t], og_s.at[t]) for t in range(2)]
-
-    def mix_stores(j, b):
-        return [
-            pltpu.make_async_copy(mix_v.at[b % 2, t], mixeds[t].at[sub_rows(b), lanes(j)], mix_s.at[b % 2, t])
-            for t in range(2)
-        ]
 
     def part_copy(j, s, k):
         return remote(
@@ -245,22 +239,13 @@
 
         @pl.when(h == 0)
         def _():
-            mix_0[sub_rows(b), :] = mixed.astype(BF16)
+            mixed_a[sub_rows(b), lanes(j)] = mixed.astype(BF16)
 
         @pl.when(h == 1)
         def _():
-            if b > 1:
-                wait_all(mix_stores(j, b))
-            else:
-
-                @pl.when(j >= 1)
-                def _():
-                    wait_all(mix_stores(j, b))
-
-            first, second = mix_0[sub_rows(b), :], mixed.astype(BF16)
+            first, second = mixed_a[sub_rows(b), lanes(j)], mixed.astype(BF16)
             for t in range(2):
-                mix_v[b % 2, t] = halves(first, second, t)
-            start_all(mix_stores(j, b))
+                mixeds[t][sub_rows(b), lanes(j)] = halves(first, second, t)
 
     first_partner, second_partner = (xp, yp), (yp, xp)
 
@@ -618,12 +603,13 @@
                         def _():
                             wait_all(wout_stores(j, t))
 
-                        wout_0[t] = both
+                        wout[t, 0] = both.astype(BF16)
 
                     @pl.when(h == 1)
                     def _():
+                        first, second = wout[t, 0], both.astype(BF16)
                         for k in range(2):
-                            wout[t, k] = halves(wout_0[t], both, k).astype(BF16)
+                            wout[t, k] = halves(first, second, k)
                         start_all(wout_stores(j, t))
 
                 @pl.when(uz < U - 2)
@@ -720,43 +706,43 @@
         copy.wait_send()
         copy.wait_recv()
     stats[...] = sred[r] + srecv[0] + srecv[1] + srecv[2]
-    for b in range(2):
-        wait_all(mix_stores(NCH - 1, b))
     for t in range(2):
         wait_all(wout_stores(NCH - 1, t))
 
 
 def hand_over(mixed_a, mixed_b, acc, wg_a, wg_b, stats, *refs):
     results, (bias_a, bias_b, stitch) = refs[:6], refs[6:9]
-    low, held, (load_s, store_s) = refs[9:11], refs[11:17], refs[17:]
-    sources = {0: mixed_a, 1: mixed_b, 4: wg_a, 5: wg_b}
-    steps = []
-    for k in (4, 0, 5, 1, 2, 3):
+    low, held, (load_s, store_s) = refs[9:11], refs[11:15], refs[15:]
+    sources = (mixed_a, mixed_b, *held)
+    loads, stores = {}, {}
+    for k in range(6):
         n = results[k].shape[0] // COPIES
         for i in range(COPIES):
             some = pl.ds(i * n, n)
-            load = None
-            if k in sources:
-                via = low[k - 4] if k >= 4 else held[k]
-                load = pltpu.make_async_copy(sources[k].at[some, :], via.at[some, :], load_s.at[k, i])
-            store = pltpu.make_async_copy(held[k].at[some, :], results[k].at[some, :], store_s.at[k, i])
-            steps.append((k, some, load, store))
-    for _, _, load, _ in steps:
-        if load is not None:
-            load.start()
+            if k >= 4:
+                src = (wg_a, wg_b)[k - 4]
+                loads[k, i] = pltpu.make_async_copy(src.at[some, :], low[k - 4].at[some, :], load_s.at[k - 4, i])
+            stores[k, i] = pltpu.make_async_copy(sources[k].at[some, :], results[k].at[some, :], store_s.at[k, i])
+    for load in loads.values():
+        load.start()
+    for (k, _), store in stores.items():
+        if k < 2:
+            store.start()
     bias_a[...] = stats[4:5, :]
     bias_b[...] = stats[5:6, :]
     stitch[0] = stats[0:2, :]
     stitch[1] = stats[2:4, :]
-    for k, some, load, store in sorted(steps, key=lambda step: (2, 3, 4, 0, 5, 1).index(step[0])):
-        if load is not None:
-            load.wait()
+    for (k, i), store in stores.items():
+        n = results[k].shape[0] // COPIES
+        some = pl.ds(i * n, n)
         if k >= 4:
-            held[k][some, :] = low[k - 4][some, :].astype(F32)
+            loads[k, i].wait()
+            held[k - 2][some, :] = low[k - 4][some, :].astype(F32)
         elif k >= 2:
-            held[k][some, :] = acc[k - 2, some, :].astype(BF16)
-        store.start()
-    for _, _, _, store in steps:
+            held[k - 2][some, :] = acc[k - 2, some, :].astype(BF16)
+        if k >= 2:
+            store.start()
+    for store in stores.values():
         store.wait()
 
 
@@ -772,15 +758,15 @@
     vmem = pl.BlockSpec(memory_space=pltpu.VMEM)
     dma = pltpu.SemaphoreType.DMA
     out_shape = (
-        jax.ShapeDtypeStruct((rows, chl), BF16),
-        jax.ShapeDtypeStruct((rows, chl), BF16),
+        pltpu.VMEM((rows, chl), BF16),
+        pltpu.VMEM((rows, chl), BF16),
         pltpu.VMEM((2, rows, width), F32),
         jax.ShapeDtypeStruct((width, 2 * chl), BF16),
         jax.ShapeDtypeStruct((width, 2 * chl), BF16),
         jax.ShapeDtypeStruct((8, LANE), F32),
     )
     results = (
-        out_shape[:2]
+        (jax.ShapeDtypeStruct((rows, chl), BF16),) * 2
         + (jax.ShapeDtypeStruct((rows, width), BF16),) * 2
         + (jax.ShapeDtypeStruct((width, 2 * chl), F32),) * 2
     )
@@ -799,13 +785,10 @@
         pltpu.VMEM((2, 2, width, LANE), BF16),
         pltpu.VMEM((2, 2, 2, width, LANE), BF16),
         pltpu.VMEM((2, 2, 3, width, LANE), BF16),
-        pltpu.VMEM((2, width, LANE), F32),
         pltpu.VMEM((2, 2, width, LANE), BF16),
         pltpu.VMEM((2, rows, LANE), BF16),
         pltpu.VMEM((rows // LANE, LANE), F32),
         pltpu.VMEM((2 * NCH, 8, LANE), F32),
-        pltpu.VMEM((rows, LANE), BF16),
-        pltpu.VMEM((2, 2, rows // NS, LANE), BF16),
         pltpu.VMEM((2 * NCH, 3, 8, LANE), F32),
         pltpu.VMEM((NCH, 8, LANE), F32),
         pltpu.VMEM((3, 8, LANE), F32),
@@ -824,7 +807,6 @@
         dma((2, 2, 3)),
         dma((2, 2)),
         dma((2,)),
-        dma((2, 2)),
         dma((3,)),
         dma((3,)),
         pltpu.SemaphoreType.REGULAR((3,)),
@@ -834,7 +816,7 @@
         functools.partial(kernel, rows, width, chl),
         out_shape=out_shape,
         in_specs=[hbm] * 4 + [vmem] * 5 + [hbm] * 2,
-        out_specs=(hbm, hbm, vmem, hbm, hbm, vmem),
+        out_specs=(vmem, vmem, vmem, hbm, hbm, vmem),
         scratch_shapes=scratch,
         compiler_params=pltpu.CompilerParams(
             collective_id=0, has_side_effects=True, vmem_limit_bytes=VMEM_LIMIT
@@ -852,8 +834,8 @@
         outgrad_a,
         outgrad_b,
     )
-    held = [pltpu.with_memory_space_constraint(v, pltpu.HBM) for v in (mixed_a, mixed_b, acc, wg_a, wg_b)]
-    held[2] = pltpu.with_memory_space_constraint(acc, pltpu.VMEM)
+    held = [pltpu.with_memory_space_constraint(v, pltpu.VMEM) for v in (mixed_a, mixed_b, acc)]
+    held += [pltpu.with_memory_space_constraint(v, pltpu.HBM) for v in (wg_a, wg_b)]
     held.append(stats)
     outs = pl.pallas_call(
         hand_over,
@@ -863,15 +845,16 @@
             jax.ShapeDtypeStruct((1, LANE), F32),
             jax.ShapeDtypeStruct((2, 2, LANE), F32),
         ),
-        in_specs=[hbm, hbm, vmem, hbm, hbm, vmem],
+        in_specs=[vmem, vmem, vmem, hbm, hbm, vmem],
         out_specs=(hbm,) * 6 + (vmem,) * 3,
-        scratch_shapes=[pltpu.VMEM(out.shape, out.dtype) for out in out_shape[3:5] + results] + [dma((6, COPIES))] * 2,
+        scratch_shapes=[pltpu.VMEM(out.shape, out.dtype) for out in out_shape[3:5] + results[2:]]
+        + [dma((2, COPIES)), dma((6, COPIES))],
         compiler_params=pltpu.CompilerParams(vmem_limit_bytes=VMEM_LIMIT),
     )(*held)
     return (*outs[:6], outs[6][0], outs[7][0], outs[8])
 
 
-VMEM_LIMIT = 52 * 1024 * 1024
+VMEM_LIMIT = 50 * 1024 * 1024
 
 
 def plain(

time: 296 us -> 294 us (level)
  no operation moved by 1% of the time
where the time goes in v7:
time: 294 us
  Pallas kernels  293 us (100%)
    pallas_call x1, Pallas kernels, fused(): pl.pallas_call(functools.partial(kernel, rows, width, chl), out_shape=out...  284 us
    pallas_call x1, Pallas kernels, fused(): pl.pallas_call(hand_over, out_shape=results + (jax.ShapeDtypeStruct((1, L...  8.84 us

profile of v7, /device:TPU:0, one launch (start us, length us, event | category | flops | bytes accessed | tf_op | source)
XLA Modules:
  0.0 293.6 jit_solution(17193723114298618190)
XLA Ops:
  0.6 283.9 %shard_map.178 = (bf16[1280,512]{1,0:T(8,128)(2,1)S(1)}, bf16[1280,512]{1,0:T(8,128)(2,1)S(1)}, f32[2,1280,1152]{2,1,0:T(8,128)S(1)}, bf16[1152,1024]{1,0:T(8,12...) custom-call(bf16[1280,1152]{1,0:T(8,128)(2,1)} %refs_0_.1, bf16[1280,1152]{1,0:T(8,128)(2,1)} %refs_1_.1, ...), custom_call_target="tpu_custom_call" | custom-call | tf_op jit(solution)/shard_map/pallas_call | solution.py:815
  284.6 8.8 %shard_map.179 = (bf16[1280,512]{1,0:T(8,128)(2,1)}, bf16[1280,512]{1,0:T(8,128)(2,1)}, bf16[1280,1152]{1,0:T(8,128)(2,1)}, bf16[1280,1152]{1,0:T(8,128)(2,1)}, ...) custom-call(bf16[1280,512]{1,0:T(8,128)(2,1)S(1)} %get-tuple-element, ...), custom_call_target="tpu_custom_call" | custom-call | tf_op jit(solution)/shard_map/pallas_call | solution.py:840

commit v8 on v7

--- a/solution.py
+++ b/solution.py
@@ -115,13 +115,13 @@
     def piece_rows(s, k):
         return pl.ds(pl.multiple_of(lax.div(s, 2) * (BIG + SMALL) + k * BIG, LANE), sizes[k])
 
-    def pool_loads(s, k):
+    def pool_loads(s, k, towers=(0, 1)):
         return [
             pltpu.make_async_copy(pools[t].at[piece_rows(s, k), :], pool_v[k].at[t], pool_s.at[k, t])
-            for t in range(2)
+            for t in towers
         ]
 
-    def wf_loads(per):
+    def wf_loads(per, towers=(0, 1)):
         j = lax.div(per, 2)
         core = jnp.where(lax.rem(per, 2) == 0, c, 1 - c)
         return [
@@ -130,7 +130,7 @@
                 wf.at[t, :, q * LANE : (q + 1) * LANE],
                 wf_s.at[t, q],
             )
-            for t in range(2)
+            for t in towers
             for q in range(L)
         ]
 
@@ -168,9 +168,9 @@
             feat=sib,
         )
 
-    def share_copy(u, o, core, d, b, s, par2):
-        block = gath.at[lax.rem(u, 4), o, core, sub_rows(b), :]
-        return remote(block, block, g_send.at[d, b, s], g_recv.at[d, b, s, par2], feat=sib)
+    def share_copy(u, o, core, d, s, par2):
+        block = gath.at[lax.rem(u, 4), o, core]
+        return remote(block, block, g_send.at[d, s], g_recv.at[d, s, par2], feat=sib)
 
     def gath_copy(u, o, d, b, s, par2):
         block = gath.at[lax.rem(u, 4), o, c, sub_rows(b), :]
@@ -291,22 +291,22 @@
         def _():
             acc[t, mine, :] += total
 
-    def first_weights():
-        out = wf_loads(0)
-        for t in range(2):
-            for q in range(L):
-                tile, k = 2 * t + q // 2, q % 2
-                out.append(
-                    pltpu.make_async_copy(
-                        weights[t].at[:, lanes((2 * q + 1 - c) * NCH)],
-                        wb.at[tile, :, k * LANE : (k + 1) * LANE],
-                        wb_s.at[tile, k],
-                    )
+    def first_weights(t):
+        out = wf_loads(0, (t,))
+        for q in range(L):
+            tile, k = 2 * t + q // 2, q % 2
+            out.append(
+                pltpu.make_async_copy(
+                    weights[t].at[:, lanes((2 * q + 1 - c) * NCH)],
+                    wb.at[tile, :, k * LANE : (k + 1) * LANE],
+                    wb_s.at[tile, k],
                 )
+            )
         return out
 
-    start_all(first_weights())
+    start_all(first_weights(0))
     start_all(pool_loads(0, 0))
+    start_all(first_weights(1))
     start_all(pool_loads(1, 1))
 
     bar = pltpu.get_barrier_semaphore()
@@ -332,16 +332,17 @@
         for k, (one, two) in enumerate(rows_of):
             par[u, k : k + 1, :] = halves(one, two, u % 2)
 
-    def first_tiles(h):
-        for t in range(2):
-            for q in range(L):
-                mine = wf[t, :, q * LANE : (q + 1) * LANE]
-                other = wb[2 * t + q // 2, :, q % 2 * LANE : (q % 2 + 1) * LANE]
-                gath[3 - h, q, t, :width, :] = halves(mine, other, h)
-
-    def first_products(h, s, k, slot):
+    def first_tiles(h, t):
+        for q in range(L):
+            mine = wf[t, :, q * LANE : (q + 1) * LANE]
+            other = wb[2 * t + q // 2, :, q % 2 * LANE : (q % 2 + 1) * LANE]
+            gath[3 - h, q, t, :width, :] = halves(mine, other, h)
+
+    def first_products(h, s, k, slot, ready=None):
         res = []
         for t in range(2):
+            if ready is not None:
+                ready(t)
             cols = jnp.concatenate([gath[3 - h, q, t, :width, :] for q in range(L)], axis=1)
             res.append(dot(pool_v[k][t], cols).astype(BF16))
         for q in range(L):
@@ -349,18 +350,23 @@
             part_own[0, h, q, piece_rows(s, k), :] = halves(*both, 0)
             part_v[k][slot, q] = halves(*both, 1)
 
-    wait_all(first_weights())
-    first_tiles(0)
+    def arrived(t):
+        wait_all(first_weights(t))
+        first_tiles(0, t)
+        wait_all(pool_loads(0, 0, (t,)))
+
     for s in range(L):
         k = s % 2
-        wait_all(pool_loads(s, k))
-        first_products(0, s, k, s // 2)
+        if s > 0:
+            wait_all(pool_loads(s, k))
+        first_products(0, s, k, s // 2, arrived if s == 0 else None)
         if s < 3:
             start_all(pool_loads((s + 2) % L, k))
         if s == 0:
             pl.semaphore_wait(bar, 4 + has_left.astype(jnp.int32) + has_right.astype(jnp.int32))
         first_copy(0, s, k).start()
-    first_tiles(1)
+    for t in range(2):
+        first_tiles(1, t)
     start_all(wf_loads(2))
 
     def begin_sums():
@@ -427,7 +433,6 @@
                 gather_here = pos[d] >= s
                 o = p - s if d == RIGHT else p + s
                 dest = p + (L - s) if d == RIGHT else p - (L - s)
-                shares = (s >= 1) if d == LEFT else (s >= 0)
 
                 @pl.when(gathers & gather_here)
                 def _():
@@ -439,10 +444,6 @@
                     def _():
                         gath_copy(u, o, d, b, s, par2).start()
 
-                    @pl.when(shares)
-                    def _():
-                        share_copy(u, o, c, d, b, s, par2).start()
-
                 begun = (ur == 0) & (s == 1)
 
                 @pl.when(sums & jnp.logical_not(gather_here | begun))
@@ -460,15 +461,23 @@
 
                     sum_copy(ur, d, b, s, par2).start()
 
+        def share_starts():
+            for d in (RIGHT, LEFT):
+                o = p - s if d == RIGHT else p + s
+                shares = (s >= 1) if d == LEFT else (s >= 0)
+
+                @pl.when(gathers & (pos[d] >= s) & shares)
+                def _():
+                    share_copy(u, o, c, d, s, par2).start()
+
         def share_waits():
-            for b in range(NS):
-                for d in (RIGHT, LEFT):
-                    o = p - s_m if d == RIGHT else p + s_m
-                    shares = (s_m >= 1) if d == LEFT else (s_m >= 0)
-
-                    @pl.when(gathers_m & (pos[d] >= s_m) & shares)
-                    def _():
-                        share_copy(u_m, o, 1 - c, d, b, s_m, par_m).wait_recv()
+            for d in (RIGHT, LEFT):
+                o = p - s_m if d == RIGHT else p + s_m
+                shares = (s_m >= 1) if d == LEFT else (s_m >= 0)
+
+                @pl.when(gathers_m & (pos[d] >= s_m) & shares)
+                def _():
+                    share_copy(u_m, o, 1 - c, d, s_m, par_m).wait_recv()
 
         def partial_products():
             @pl.when(per < U)
@@ -637,16 +646,17 @@
             start_all(wb_loads(jp, 0))
 
         flows(0)
+        flows(1)
         share_waits()
         weight_products(0)
-        flows(1)
-        pool_piece(0)
         flows(2)
         send_near()
         weight_products(1)
         flows(3)
+        pool_piece(0)
+        flows(4)
+        share_starts()
         pool_piece(1)
-        flows(4)
         partial_products()
         finish_weights()
 
@@ -656,19 +666,19 @@
             def _():
                 part_copy(0, s_m, k).wait_send()
 
+        for d in (RIGHT, LEFT):
+            shares = (s_m >= 1) if d == LEFT else (s_m >= 0)
+
+            @pl.when(gathers_m & (pos[d] >= s_m) & shares)
+            def _():
+                share_copy(u_m, p, c, d, s_m, par_m).wait_send()
+
         for b in range(NS):
             for d in (RIGHT, LEFT):
-                shares = (s_m >= 1) if d == LEFT else (s_m >= 0)
-
-                @pl.when(gathers_m & (pos[d] >= s_m))
+
+                @pl.when(gathers_m & (pos[d] >= s_m) & (pos[d] < L - 1))
                 def _():
-                    @pl.when(pos[d] < L - 1)
-                    def _():
-                        gath_copy(u_m, p, d, b, s_m, par_m).wait_send()
-
-                    @pl.when(shares)
-                    def _():
-                        share_copy(u_m, p, c, d, b, s_m, par_m).wait_send()
+                    gath_copy(u_m, p, d, b, s_m, par_m).wait_send()
 
                 @pl.when(sums_m & (pos[d] < s_m))
                 def _():
@@ -801,8 +811,8 @@
         dma((2, L)),
         dma((2, NS, L)),
         dma((2, NS, L, 2)),
-        dma((2, NS, L)),
-        dma((2, NS, L, 2)),
+        dma((2, L)),
+        dma((2, L, 2)),
         dma((2, 3)),
         dma((2, 2, 3)),
         dma((2, 2)),

time: 294 us -> 292 us (level)
  no operation moved by 1% of the time
where the time goes in v8:
time: 292 us
  Pallas kernels  291 us (100%)
    pallas_call x1, Pallas kernels, fused(): pl.pallas_call(functools.partial(kernel, rows, width, chl), out_shape=out...  282 us
    pallas_call x1, Pallas kernels, fused(): pl.pallas_call(hand_over, out_shape=results + (jax.ShapeDtypeStruct((1, L...  8.84 us

profile of v8, /device:TPU:0, one launch (start us, length us, event | category | flops | bytes accessed | tf_op | source)
XLA Modules:
  0.0 292.0 jit_solution(14018892637938707600)
XLA Ops:
  0.6 282.4 %shard_map.178 = (bf16[1280,512]{1,0:T(8,128)(2,1)S(1)}, bf16[1280,512]{1,0:T(8,128)(2,1)S(1)}, f32[2,1280,1152]{2,1,0:T(8,128)S(1)}, bf16[1152,1024]{1,0:T(8,12...) custom-call(bf16[1280,1152]{1,0:T(8,128)(2,1)} %refs_0_.1, bf16[1280,1152]{1,0:T(8,128)(2,1)} %refs_1_.1, ...), custom_call_target="tpu_custom_call" | custom-call | tf_op jit(solution)/shard_map/pallas_call | solution.py:825
  283.0 8.8 %shard_map.179 = (bf16[1280,512]{1,0:T(8,128)(2,1)}, bf16[1280,512]{1,0:T(8,128)(2,1)}, bf16[1280,1152]{1,0:T(8,128)(2,1)}, bf16[1280,1152]{1,0:T(8,128)(2,1)}, ...) custom-call(bf16[1280,512]{1,0:T(8,128)(2,1)S(1)} %get-tuple-element, ...), custom_call_target="tpu_custom_call" | custom-call | tf_op jit(solution)/shard_map/pallas_call | solution.py:850

commit v9 on v8

--- a/solution.py
+++ b/solution.py
@@ -491,15 +491,15 @@
 
                         @pl.when(per == 2)
                         def _():
+                            if k == 0:
+
+                                @pl.when(s == 0)
+                                def _():
+                                    begin_sums()
+
                             first_copy(0, s, k).wait_send()
                             first_products(1, s, k, lax.div(s, 2))
                             first_copy(1, s, k).start()
-                            if k == 0:
-
-                                @pl.when(s == 0)
-                                def _():
-                                    begin_sums()
-
                         if k == 0:
 
                             @pl.when(s == 0)
@@ -590,7 +590,7 @@
                 pool_products(jp, 1, 2 * (s - 1) + k)
 
         def send_near():
-            @pl.when((s == 2) & (ub >= 0) & (ub < U))
+            @pl.when((s == 1) & (ub >= 0) & (ub < U))
             def _():
                 for t in range(2):
                     w_copy(ub, t, NEAR).start()

time: 292 us -> 292 us (level)
  no operation moved by 1% of the time
where the time goes in v9:
time: 292 us
  Pallas kernels  291 us (100%)
    pallas_call x1, Pallas kernels, fused(): pl.pallas_call(functools.partial(kernel, rows, width, chl), out_shape=out...  282 us
    pallas_call x1, Pallas kernels, fused(): pl.pallas_call(hand_over, out_shape=results + (jax.ShapeDtypeStruct((1, L...  8.84 us

profile of v9, /device:TPU:0, one launch (start us, length us, event | category | flops | bytes accessed | tf_op | source)
XLA Modules:
  0.0 291.9 jit_solution(10968379562120610917)
XLA Ops:
  0.6 282.3 %shard_map.178 = (bf16[1280,512]{1,0:T(8,128)(2,1)S(1)}, bf16[1280,512]{1,0:T(8,128)(2,1)S(1)}, f32[2,1280,1152]{2,1,0:T(8,128)S(1)}, bf16[1152,1024]{1,0:T(8,12...) custom-call(bf16[1280,1152]{1,0:T(8,128)(2,1)} %refs_0_.1, bf16[1280,1152]{1,0:T(8,128)(2,1)} %refs_1_.1, ...), custom_call_target="tpu_custom_call" | custom-call | tf_op jit(solution)/shard_map/pallas_call | solution.py:825
  282.9 8.8 %shard_map.179 = (bf16[1280,512]{1,0:T(8,128)(2,1)}, bf16[1280,512]{1,0:T(8,128)(2,1)}, bf16[1280,1152]{1,0:T(8,128)(2,1)}, bf16[1280,1152]{1,0:T(8,128)(2,1)}, ...) custom-call(bf16[1280,512]{1,0:T(8,128)(2,1)S(1)} %get-tuple-element, ...), custom_call_target="tpu_custom_call" | custom-call | tf_op jit(solution)/shard_map/pallas_call | solution.py:850
